TPU v7x, 256 devices: a whole 4x4x8 slice. The times are simulated.
256 devices in a mesh: grp: 16 (over x_hi, z), blk: 16 (over x_lo, y, core).
Axes of the slice: x: 4 (x_hi: 2, x_lo: 2; x = x_hi * 2 + x_lo), y: 4, z: 8, core: 2. Of those that a mesh axis runs over, the one named last changes fastest.
Arguments:
- prompt_of: int32 [2048], P(('grp', 'blk')), may hold values from 0 to 31, as said below
- suffix_len: int32 [2048], P(('grp', 'blk')), may hold values from 1 to 256, as said below
- query: bfloat16 [2048, 4096], P(('grp', 'blk')), may hold values from -8 to 23
- new_key: bfloat16 [2048, 512], P(('grp', 'blk')), may hold values from -5 to 6
- new_value: bfloat16 [2048, 512], P(('grp', 'blk')), may hold values from -6 to 6
- suffix_key: bfloat16 [2048, 256, 512], P(('grp', 'blk')), may hold values from -5 to 6
- suffix_value: bfloat16 [2048, 256, 512], P(('grp', 'blk')), may hold values from -6 to 6
- prefix_key: bfloat16 [32, 4096, 512], P('grp', 'blk'), may hold values from -5 to 6
- prefix_value: bfloat16 [32, 4096, 512], P('grp', 'blk'), may hold values from -6 to 6
Outputs:
- attended: bfloat16 [2048, 4096], P(('grp', 'blk'))
Inputs may be any that keep to these rules, and one draw needn't show every extreme that they name: `prompt_of`: on every device at most 2 of its completions name prompts of one group (the group of a prompt is prompt // 2); one group gets exactly 2 from every device. `suffix_len`: some completion has exactly 256 cached suffix tokens.
All inputs are finite; a program needn't handle non-finite values.
Results may differ from a plain program's by a relative error of at most 0.0037.
Values may be sent and summed in bfloat16 or wider, within the bound.
No kernel may reach another device: no remote copies, remote signals or barrier semaphores. Data moves between devices by JAX's collectives and lax.ppermute only.
A program may use at most 128 MiB of HBM per device.

v0:
```python
import jax
import jax.numpy as jnp
from jax import lax
from jax.sharding import PartitionSpec as P

HD = 128
CAP = 2


NEG = -1e30


def shards(
    prompt_of,
    suffix_len,
    query,
    new_key,
    new_value,
    suffix_key,
    suffix_value,
    prefix_key,
    prefix_value,
):
    groups = lax.axis_size("grp")
    held_count = query.shape[0]
    row_width = query.shape[1]
    kv_heads = new_key.shape[1] // HD
    query_heads = row_width // HD
    group_ratio = query_heads // kv_heads
    per_group = prefix_key.shape[0]
    suffix_cap = suffix_key.shape[1]
    slot_count = groups * CAP
    scaling = HD ** (-0.5)
    owners = prompt_of // per_group
    local_prompt = prompt_of % per_group
    positions = jnp.arange(held_count)
    earlier = (owners[:, None] == owners[None, :]) & (positions[None, :] < positions[:, None])
    slot_rank = jnp.sum(earlier.astype(jnp.int32), axis=1)
    slot_of = owners * CAP + slot_rank
    select = jnp.arange(slot_count)[:, None] == slot_of[None, :]
    outgoing = jnp.dot(
        select.astype(jnp.bfloat16), query, preferred_element_type=jnp.float32
    ).astype(jnp.bfloat16)
    outgoing_tags = jnp.sum(jnp.where(select, local_prompt[None, :] + 1, 0), axis=1)
    arrived, arrived_tags = (
        lax.all_to_all(
            outgoing.reshape(groups, CAP, row_width), "grp", split_axis=0, concat_axis=0, tiled=True
        ),
        lax.all_to_all(
            outgoing_tags.reshape(groups, CAP), "grp", split_axis=0, concat_axis=0, tiled=True
        ),
    )
    slot_rows = arrived.reshape(slot_count, row_width)
    slot_tags = arrived_tags.reshape(slot_count)

    def masked_scores(query_block, tag_block, key_piece):
        piece_len = key_piece.shape[1]
        key_heads = key_piece.reshape(-1, kv_heads, HD)
        key_prompt = jnp.arange(key_heads.shape[0]) // piece_len
        heads_view = query_block.reshape(query_block.shape[0], kv_heads, group_ratio, HD)
        scores = (
            jnp.einsum("rkgd,tkd->rkgt", heads_view, key_heads, preferred_element_type=jnp.float32)
            * scaling
        )
        allowed = (key_prompt[None, :] == tag_block[:, None] - 1) | (tag_block[:, None] == 0)
        return jnp.where(allowed[:, None, None, :], scores, NEG)

    def weighted_sums(scores, top_rows, value_piece):
        rows = scores.shape[0]
        value_heads = value_piece.reshape(-1, kv_heads, HD)
        weights = jnp.exp(scores - top_rows.reshape(rows, kv_heads, group_ratio)[:, :, :, None])
        row_total = jnp.sum(weights, axis=3).reshape(rows, query_heads)
        mixed_out = jnp.einsum(
            "rkgt,tkd->rkgd",
            weights.astype(jnp.bfloat16),
            value_heads,
            preferred_element_type=jnp.float32,
        )
        return (row_total, mixed_out.reshape(rows, row_width))

    every_query, every_tag = (
        lax.all_gather(slot_rows, "blk", axis=0, tiled=True),
        lax.all_gather(slot_tags, "blk", axis=0, tiled=True),
    )
    total_rows = every_query.shape[0]
    block_rows = 128
    query_blocks = every_query.reshape(-1, block_rows, row_width)
    tag_blocks = every_tag.reshape(-1, block_rows)

    def block_peak(pieces):
        query_block, tag_block = pieces
        scores = masked_scores(query_block, tag_block, prefix_key)
        return jnp.max(scores, axis=3).reshape(block_rows, query_heads)

    local_max = lax.map(block_peak, (query_blocks, tag_blocks)).reshape(total_rows, query_heads)
    global_max = lax.pmax(local_max, "blk")

    def block_sums(pieces):
        query_block, tag_block, top_block = pieces
        scores = masked_scores(query_block, tag_block, prefix_key)
        return weighted_sums(scores, top_block, prefix_value)

    local_total, local_out = lax.map(
        block_sums, (query_blocks, tag_blocks, global_max.reshape(-1, block_rows, query_heads))
    )
    far_out, far_total = (
        lax.psum_scatter(
            local_out.reshape(total_rows, row_width), "blk", scatter_dimension=0, tiled=True
        ),
        lax.psum_scatter(
            local_total.reshape(total_rows, query_heads), "blk", scatter_dimension=0, tiled=True
        ),
    )
    far_max = lax.dynamic_slice_in_dim(
        global_max, lax.axis_index("blk") * slot_count, slot_count, 0
    )
    back_out, back_total, back_max = (
        lax.all_to_all(
            far_out.reshape(groups, CAP, row_width), "grp", split_axis=0, concat_axis=0, tiled=True
        ),
        lax.all_to_all(
            far_total.reshape(groups, CAP, query_heads),
            "grp",
            split_axis=0,
            concat_axis=0,
            tiled=True,
        ),
        lax.all_to_all(
            far_max.reshape(groups, CAP, query_heads),
            "grp",
            split_axis=0,
            concat_axis=0,
            tiled=True,
        ),
    )
    mine_out = jnp.take(back_out.reshape(slot_count, row_width), slot_of, axis=0).reshape(
        held_count, kv_heads, group_ratio, HD
    )
    mine_total = jnp.take(back_total.reshape(slot_count, query_heads), slot_of, axis=0).reshape(
        held_count, kv_heads, group_ratio
    )
    mine_max = jnp.take(back_max.reshape(slot_count, query_heads), slot_of, axis=0).reshape(
        held_count, kv_heads, group_ratio
    )
    own_heads = query.reshape(held_count, kv_heads, group_ratio, HD)
    cache_keys = suffix_key.reshape(held_count, suffix_cap, kv_heads, HD)
    cache_values = suffix_value.reshape(held_count, suffix_cap, kv_heads, HD)
    near_scores = (
        jnp.einsum("ckgd,ctkd->ckgt", own_heads, cache_keys, preferred_element_type=jnp.float32)
        * scaling
    )
    live_mask = jnp.arange(suffix_cap)[None, :] < suffix_len[:, None]
    near_scores = jnp.where(live_mask[:, None, None, :], near_scores, NEG)
    own_score = (
        jnp.einsum(
            "ckgd,ckd->ckg",
            own_heads,
            new_key.reshape(held_count, kv_heads, HD),
            preferred_element_type=jnp.float32,
        )
        * scaling
    )
    near_max = jnp.maximum(jnp.max(near_scores, axis=3), own_score)
    near_weights = jnp.where(
        live_mask[:, None, None, :], jnp.exp(near_scores - near_max[:, :, :, None]), 0.0
    )
    own_weight = jnp.exp(own_score - near_max)
    near_total = jnp.sum(near_weights, axis=3) + own_weight
    near_out = jnp.einsum(
        "ckgt,ctkd->ckgd",
        near_weights.astype(jnp.bfloat16),
        cache_values,
        preferred_element_type=jnp.float32,
    )
    own_rounded = lax.optimization_barrier(own_weight.astype(jnp.bfloat16)).astype(jnp.float32)
    near_out = near_out + own_rounded[:, :, :, None] * new_value.reshape(
        held_count, kv_heads, 1, HD
    ).astype(jnp.float32)
    top_max = jnp.maximum(mine_max, near_max)
    far_scale = jnp.exp(mine_max - top_max)
    near_scale = jnp.exp(near_max - top_max)
    numerator = mine_out * far_scale[:, :, :, None] + near_out * near_scale[:, :, :, None]
    denominator = mine_total * far_scale + near_total * near_scale
    return (
        (numerator / denominator[:, :, :, None]).reshape(held_count, row_width).astype(jnp.bfloat16)
    )


def solution(mesh):
    in_specs = (
        P(("grp", "blk")),
        P(("grp", "blk")),
        P(("grp", "blk"), None),
        P(("grp", "blk"), None),
        P(("grp", "blk"), None),
        P(("grp", "blk"), None, None),
        P(("grp", "blk"), None, None),
        P("grp", "blk", None),
        P("grp", "blk", None),
    )
    out_specs = P(("grp", "blk"), None)
    return jax.shard_map(shards, mesh=mesh, in_specs=in_specs, out_specs=out_specs, check_vma=False)
```

profile of v0, /device:TPU:32, one launch (start us, length us, event | category | flops | bytes accessed | tf_op | source)
XLA Modules:
  0.0 438.7 jit_solution(16554184321360019398)
XLA Ops:
  8.9 22.4 %all_to_all.29 = bf16[16,2,4096]{2,1,0:T(2,128)(2,1)S(1)} all-to-all(bf16[16,2,4096]{2,1,0:T(2,128)(2,1)S(1)} %reshape.326), channel_id=1, replica_groups=mesh['grp'=16,'blk'=16] {'grp'}, dimensions={0} | all-to-all | bytes 524288 | tf_op jit(solution)/shard_map/all_to_all | solution.py:46
  32.9 4.6 %all-to-all-start = ((s32[16,1,2]{2,1,0:T(1,128)}), s32[16,1,2]{2,1,0:T(1,128)S(1)}, u32[]{:S(2)}, u32[]{:S(2)}) async-start(s32[16,1,2]{2,1,0:T(1,128)} %bitcast.16), calls=%async_computation | async-start | bytes 16384 | tf_op jit(solution)/shard_map/all_to_all | solution.py:49
  40.7 5.3 %all-to-all-done = s32[16,1,2]{2,1,0:T(1,128)S(1)} async-done(((s32[16,1,2]{2,1,0:T(1,128)}), s32[16,1,2]{2,1,0:T(1,128)S(1)}, u32[]{:S(2)}, u32[]{:S(2)}) %all-to-all-start) | async-done | bytes 160 | tf_op jit(solution)/shard_map/all_to_all | solution.py:49
  47.6 11.7 %all-reduce = s32[512]{0:T(512)S(1)} all-reduce(s32[512]{0:T(512)S(1)} %dynamic-update-slice), channel_id=1, replica_groups=mesh['grp'=16,'blk'=16] {'blk'}, use_global_device_ids=true, to_apply=%add | all-reduce | flops 512 | bytes 4096
  59.2 9.1 %all-gather.2.cloned.1.call-done = bf16[512,4096]{1,0:T(8,128)(2,1)} async-done(((bf16[32,4096]{1,0:T(8,128)(2,1)}), bf16[512,4096]{1,0:T(8,128)(2,1)}) %all-gather.2.cloned.1.call-update) | async-done | bytes 4194320 | tf_op jit(solution)/shard_map/all_gather | solution.py:82
  68.4 6.3 %copy.87 = bf16[4,128,4096]{1,2,0:T(8,128)(2,1)} copy(bf16[4,128,4096]{2,1,0:T(8,128)(2,1)} %bitcast.171) | data formatting | bytes 8388608 | tf_op jit(solution)/shard_map/while | solution.py:103
  74.7 13.6 %while.30 = (s32[]{:T(128)}, f32[4,128,32]{1,0,2:T(4,128)S(1)}, s32[4,128]{1,0:T(4,128)S(1)}, bf16[4,128,4096]{1,2,0:T(8,128)(2,1)}, bf16[2,256,512]{2,1,0:T(8,1...) while((s32[]{:T(128)}, f32[4,128,32]{1,0,2:T(4,128)S(1)}, ...), condition=%wide.wide.region_4.5_spmd, body=%wide.wide.region_2.4_spmd.sunk | while | flops 543293696 | bytes 3856741 | solution.py:95
  91.8 108.3 %all-reduce.3.cloned.1.call-done = f32[512,32]{0,1:T(8,128)} async-done(((f32[512,32]{0,1:T(8,128)}), f32[512,32]{0,1:T(8,128)}) %all-reduce.3.cloned.1.call-update) | async-done | bytes 65552 | tf_op jit(solution)/shard_map/pmax | solution.py:96
  200.9 59.8 %while.31 = (s32[]{:T(128)}, f32[4,128,32]{1,2,0:T(8,128)S(1)}, f32[4,128,4096]{2,1,0:T(8,128)}, s32[4,128]{1,0:T(4,128)S(1)}, bf16[4,128,4096]{1,2,0:T(8,128)(2...) while((s32[]{:T(128)}, f32[4,128,32]{1,2,0:T(8,128)S(1)}, ...), condition=%wide.wide.region_8.9_spmd, body=%wide.wide.region_6.8_spmd.sunk | while | flops 1090650368 | bytes 31775616 | solution.py:103
  202.4 4.0 fusion.96
  206.4 3.4 fusion.97
  209.9 2.9 copy.177
  212.8 3.1 constant_dynamic-update-slice_fusion.3
  217.4 4.0 fusion.96
  221.4 3.4 fusion.97
  224.8 2.9 copy.177
  227.7 3.1 constant_dynamic-update-slice_fusion.3
  232.3 4.0 fusion.96
  236.3 3.4 fusion.97
  239.7 2.9 copy.177
  242.6 3.1 constant_dynamic-update-slice_fusion.3
  247.2 4.0 fusion.96
  251.2 3.4 fusion.97
  254.7 2.9 copy.177
  257.6 3.1 constant_dynamic-update-slice_fusion.3
  264.5 9.9 %all-to-all-start.3 = ((f32[16,2,32]{2,1,0:T(2,128)}), f32[16,2,32]{2,1,0:T(2,128)S(1)}, u32[]{:S(2)}, u32[]{:S(2)}) async-start(f32[16,2,32]{2,1,0:T(2,128)} %bitcast.21), calls=%async_computation.4 | async-start | bytes 32768 | tf_op jit(solution)/shard_map/all_to_all | solution.py:128
  274.6 8.5 %all-to-all-done.3 = f32[16,2,32]{2,1,0:T(2,128)S(1)} async-done(((f32[16,2,32]{2,1,0:T(2,128)}), f32[16,2,32]{2,1,0:T(2,128)S(1)}, u32[]{:S(2)}, u32[]{:S(2)}) %all-to-all-start.3) | async-done | bytes 4128 | tf_op jit(solution)/shard_map/all_to_all | solution.py:128
  283.1 42.9 %reduce-scatter.7.cloned.1.call-done = f32[32,32]{1,0:T(8,128)} async-done(((f32[512,32]{1,0:T(8,128)}), f32[32,32]{1,0:T(8,128)}) %reduce-scatter.7.cloned.1.call-update) | async-done | bytes 4112 | tf_op jit(solution)/shard_map/reduce_scatter | solution.py:110
  326.0 9.5 %all-to-all-start.4 = ((f32[16,2,32]{2,1,0:T(2,128)}), f32[16,2,32]{2,1,0:T(2,128)S(1)}, u32[]{:S(2)}, u32[]{:S(2)}) async-start(f32[16,2,32]{2,1,0:T(2,128)} %bitcast.187), calls=%async_computation.5 | async-start | bytes 32768 | tf_op jit(solution)/shard_map/all_to_all | solution.py:121
  335.5 68.6 %reduce-scatter.5.cloned.1.call-done = f32[32,4096]{1,0:T(8,128)} async-done(((f32[512,4096]{1,0:T(8,128)}), f32[32,4096]{1,0:T(8,128)}) %reduce-scatter.5.cloned.1.call-update) | async-done | bytes 524304 | tf_op jit(solution)/shard_map/reduce_scatter | solution.py:107
  406.2 9.6 %all-to-all-start.2 = ((f32[16,2,4096]{2,1,0:T(2,128)}), f32[16,2,4096]{2,1,0:T(2,128)S(1)}, u32[]{:S(2)}, u32[]{:S(2)}) async-start(f32[16,2,4096]{2,1,0:T(2,128)} %reshape.332), calls=%async_computation.3 | async-start | bytes 1048576 | tf_op jit(solution)/shard_map/all_to_all | solution.py:118
  417.5 11.0 %all-to-all-done.2 = f32[16,2,4096]{2,1,0:T(2,128)S(1)} async-done(((f32[16,2,4096]{2,1,0:T(2,128)}), f32[16,2,4096]{2,1,0:T(2,128)S(1)}, u32[]{:S(2)}, u32[]{:S(2)}) %all-to-all-start.2) | async-done | bytes 524320 | tf_op jit(solution)/shard_map/all_to_all | solution.py:118
  (126 shorter events, 42.9 us)
Async XLA Ops:
  6.5 255.7 %copy-start = (bf16[8,256,512]{2,1,0:T(8,128)(2,1)S(1)}, bf16[8,256,512]{2,1,0:T(8,128)(2,1)}, u32[]{:S(2)}) copy-start(bf16[8,256,512]{2,1,0:T(8,128)(2,1)} %param.20) | copy-start | bytes 6291460
  6.5 61.8 %all-gather.2.cloned.1.call-start = ((), (), s32[]{:S(2)}) async-start(), calls=%async_computation.7 | async-start | bytes 4456448 | tf_op jit(solution)/shard_map/all_gather | solution.py:82
  32.9 13.1 %all-to-all-start = ((s32[16,1,2]{2,1,0:T(1,128)}), s32[16,1,2]{2,1,0:T(1,128)S(1)}, u32[]{:S(2)}, u32[]{:S(2)}) async-start(s32[16,1,2]{2,1,0:T(1,128)} %bitcast.16), calls=%async_computation | async-start | bytes 16384 | tf_op jit(solution)/shard_map/all_to_all | solution.py:49
  37.5 162.6 %all-reduce.3.cloned.1.call-start = ((), (), s32[]{:S(2)}) async-start(), calls=%async_computation.8 | async-start | bytes 131072 | tf_op jit(solution)/shard_map/pmax | solution.py:96
  74.7 16.3 %copy-start.2 = (bf16[2,256,512]{2,1,0:T(8,128)(2,1)S(1)}, bf16[2,256,512]{2,1,0:T(8,128)(2,1)}, u32[]{:S(2)}) copy-start(bf16[2,256,512]{2,1,0:T(8,128)(2,1)} %param.23) | copy-start | bytes 1572868
  88.9 237.0 %reduce-scatter.7.cloned.1.call-start = ((), (), s32[]{:S(2)}) async-start(), calls=%async_computation.10 | async-start | bytes 278528 | tf_op jit(solution)/shard_map/reduce_scatter | solution.py:110
  91.4 109.5 %copy-start.1 = (bf16[2,256,512]{1,0,2:T(2,128)(2,1)}, bf16[2,256,512]{1,0,2:T(2,128)(2,1)S(1)}, u32[]{:S(2)}) copy-start(bf16[2,256,512]{1,0,2:T(2,128)(2,1)S(1)} %copy.89) | copy-start | bytes 1572868
  260.7 1.5 copy-start.5
  260.7 1.6 copy-start.3
  260.7 13.7 %copy-start.6 = (bf16[8,512]{1,0:T(8,128)(2,1)S(1)}, bf16[8,512]{1,0:T(8,128)(2,1)}, u32[]{:S(2)}) copy-start(bf16[8,512]{1,0:T(8,128)(2,1)} %param.18) | copy-start | bytes 24580
  260.7 155.1 %copy-start.4 = (bf16[8,512]{1,0:T(8,128)(2,1)S(1)}, bf16[8,512]{1,0:T(8,128)(2,1)}, u32[]{:S(2)}) copy-start(bf16[8,512]{1,0:T(8,128)(2,1)} %param.19) | copy-start | bytes 24580
  261.6 142.4 %reduce-scatter.5.cloned.1.call-start = ((), (), s32[]{:S(2)}) async-start(), calls=%async_computation.9 | async-start | bytes 8912896 | tf_op jit(solution)/shard_map/reduce_scatter | solution.py:107
  264.5 18.6 %all-to-all-start.3 = ((f32[16,2,32]{2,1,0:T(2,128)}), f32[16,2,32]{2,1,0:T(2,128)S(1)}, u32[]{:S(2)}, u32[]{:S(2)}) async-start(f32[16,2,32]{2,1,0:T(2,128)} %bitcast.21), calls=%async_computation.4 | async-start | bytes 32768 | tf_op jit(solution)/shard_map/all_to_all | solution.py:128
  326.0 80.2 %all-to-all-start.4 = ((f32[16,2,32]{2,1,0:T(2,128)}), f32[16,2,32]{2,1,0:T(2,128)S(1)}, u32[]{:S(2)}, u32[]{:S(2)}) async-start(f32[16,2,32]{2,1,0:T(2,128)} %bitcast.187), calls=%async_computation.5 | async-start | bytes 32768 | tf_op jit(solution)/shard_map/all_to_all | solution.py:121
  406.2 22.3 %all-to-all-start.2 = ((f32[16,2,4096]{2,1,0:T(2,128)}), f32[16,2,4096]{2,1,0:T(2,128)S(1)}, u32[]{:S(2)}, u32[]{:S(2)}) async-start(f32[16,2,4096]{2,1,0:T(2,128)} %reshape.332), calls=%async_computation.3 | async-start | bytes 1048576 | tf_op jit(solution)/shard_map/all_to_all | solution.py:118
Sparse Core Ops, SparseCore 0:
  32.3 36.0 all-gather.1
  89.1 110.9 all-reduce.2
  261.7 64.2 reduce-scatter.6
  328.4 75.5 reduce-scatter.4
where the time goes:
time: 442 us; the launch traced here: 439 us
  waiting for transfers between devices  254 us (57%)
  local copies, waits for them, and re-layouts  57.9 us (13%)
  matrix products  41.1 us (9%)
  blocking collectives  34.1 us (8%)
  starting transfers between devices  33.7 us (8%)
  between operations  14 us (3%)
    pmax x1, waiting for transfers between devices, shards(): global_max = lax.pmax(local_max, 'blk')  108 us
    reduce_scatter x1, waiting for transfers between devices, shards(): lax.psum_scatter(local_out.reshape(total_rows, row_width), 'blk', scatter...  68.6 us
    reduce_scatter x1, waiting for transfers between devices, shards(): lax.psum_scatter(local_total.reshape(total_rows, query_heads), 'blk', sca...  42.9 us
    dynamic_update_slice x8, local copies, waits for them, and re-layouts, shards(): lax.map(block_sums, (query_blocks, tag_blocks, global_max.reshape(-1, blo...  24.1 us
    dot_general x8, matrix products, masked_scores(): jnp.einsum('rkgd,tkd->rkgt', heads_view, key_heads, preferred_element_typ...  23.2 us
    all_to_all x1, blocking collectives, shards(): lax.all_to_all(outgoing.reshape(groups, CAP, row_width), 'grp', split_axi...  22.4 us
    dot_general x4, matrix products, weighted_sums(): jnp.einsum('rkgt,tkd->rkgd', weights.astype(jnp.bfloat16), value_heads, p...  13.7 us
    unnamed x1, blocking collectives  11.7 us
  transfers between devices with their start and end apart: 8, of which 7 were waited for; matrix products, arithmetic and copies ran while one was open for 3% of the time, Pallas kernels for 0%

commit v1 on v0

v1 whole, which is shorter than its diff:
```python
import jax
import jax.numpy as jnp
from jax import lax
from jax.experimental import pallas as pl
from jax.experimental.pallas import tpu as pltpu
from jax.sharding import Mesh, PartitionSpec as P

HD = 128
CAP = 2
HELD = 8
HEADS = 32
KVH = 4
RATIO = 8
PROMPTS = 32
PARTS = 8
PART_HEADS = 4
DEVICES = 256
SUF = 256
PIECE = 256
ROWS = DEVICES * CAP * PART_HEADS
NEG = -1e30
SCALE = HD ** (-0.5)
LOG2E = 1.4426950408889634
LN2 = 0.6931471805599453
ALL = ("xh", "z", "xl", "y", "c")
NEAR = ("xl", "y")


def slots_of(prompt_ref):
    prompts = [prompt_ref[i] for i in range(HELD)]
    slots = []
    for i in range(HELD):
        rank = jnp.int32(0)
        for j in range(i):
            rank = rank + jnp.where(prompts[j] == prompts[i], 1, 0)
        slots.append(prompts[i] * CAP + rank)
    return slots


def spread(values, index):
    picked = jnp.zeros(index.shape, jnp.int32)
    for i, value in enumerate(values):
        picked = jnp.where(index == i, value, picked)
    return picked


def pack_kernel(prompt_ref, query_ref, out_ref):
    slots = slots_of(prompt_ref)
    held = jnp.concatenate(
        [query_ref[:, h * HD : (h + 1) * HD].astype(jnp.float32) for h in range(HEADS)], axis=0
    ).astype(jnp.bfloat16)
    lane = lax.broadcasted_iota(jnp.int32, (1, HEADS * HELD), 1)
    lane_key = (lane >> 3) * 64 + spread(slots, lane & 7)
    chunk = 512
    for start in range(0, ROWS, chunk):
        row = lax.broadcasted_iota(jnp.int32, (chunk, 1), 0) + start
        head = ((row >> 3) & 7) * 4 + (row & 3)
        slot = (row >> 6) * 2 + ((row >> 2) & 1)
        select = (head * 64 + slot == lane_key).astype(jnp.float32).astype(jnp.bfloat16)
        out_ref[start : start + chunk, :] = jnp.dot(
            select, held, preferred_element_type=jnp.float32
        ).astype(jnp.bfloat16)


def cut_kernel(place_ref, key_ref, value_ref, *out_refs):
    place = place_ref[0]
    for step, out_ref in enumerate(out_refs):
        target = place ^ step
        prompt = target >> 2
        column = pl.multiple_of((target & 3) * HD, HD)
        out_ref[0] = key_ref[prompt, :, pl.ds(column, HD)]
        out_ref[1] = value_ref[prompt, :, pl.ds(column, HD)]


def near_kernel(len_ref, query_ref, new_key_ref, new_value_ref, key_ref, value_ref, out_ref, lse_ref):
    step = pl.program_id(0)
    length = len_ref[step]
    query = query_ref[0]
    keys = key_ref[0]
    values = value_ref[0]
    new_key = new_key_ref[pl.ds(step, 1), :]
    new_value = new_value_ref[pl.ds(step, 1), :]

    def spread_heads(row):
        return jnp.concatenate(
            [jnp.broadcast_to(row[:, k * HD : (k + 1) * HD], (RATIO, HD)) for k in range(KVH)], axis=0
        )

    scores = jnp.concatenate(
        [
            lax.dot_general(
                query,
                keys[:, k * HD : (k + 1) * HD],
                (((1,), (1,)), ((), ())),
                preferred_element_type=jnp.float32,
            )[k * RATIO : (k + 1) * RATIO]
            for k in range(KVH)
        ],
        axis=0,
    ) * SCALE
    own = jnp.sum(query.astype(jnp.float32) * spread_heads(new_key), axis=1, keepdims=True) * SCALE
    live = lax.broadcasted_iota(jnp.int32, (1, SUF), 1) < length
    scores = jnp.where(live, scores, NEG)
    top = jnp.maximum(jnp.max(scores, axis=1, keepdims=True), own)
    weights = jnp.where(live, jnp.exp(scores - top), 0.0)
    own_weight = jnp.exp(own - top)
    total = jnp.sum(weights, axis=1, keepdims=True) + own_weight
    rounded = weights.astype(jnp.bfloat16)
    mixed = jnp.concatenate(
        [
            jnp.dot(rounded, values[:, k * HD : (k + 1) * HD], preferred_element_type=jnp.float32)[
                k * RATIO : (k + 1) * RATIO
            ]
            for k in range(KVH)
        ],
        axis=0,
    )
    mixed = mixed + own_weight.astype(jnp.bfloat16).astype(jnp.float32) * spread_heads(new_value)
    out_ref[:, pl.ds(step, 1), :] = (mixed / total).reshape(HEADS, 1, HD)
    lse_ref[:, pl.ds(step, 1), :] = jnp.broadcast_to(top + jnp.log(total), (HEADS, HD)).reshape(
        HEADS, 1, HD
    )


def far_kernel(query_ref, *refs):
    pieces = refs[:-3]
    out_ref, stat_ref, score_ref = refs[-3:]
    block = 256

    @pl.loop(0, ROWS // block)
    def _(index):
        start = pl.multiple_of(index * block, block)
        query = query_ref[pl.ds(start, block), :]
        peak = jnp.full((block, HD), -jnp.inf, jnp.float32)
        for n, piece in enumerate(pieces):
            scores = lax.dot_general(
                query, piece[0], (((1,), (1,)), ((), ())), preferred_element_type=jnp.float32
            )
            score_ref[n] = scores
            peak = jnp.maximum(peak, jnp.maximum(scores[:, :HD], scores[:, HD:]))
        peak = jnp.max(peak, axis=1, keepdims=True)
        total = jnp.zeros((block, HD), jnp.float32)
        mixed = jnp.zeros((block, HD), jnp.float32)
        for n, piece in enumerate(pieces):
            weights = jnp.exp2((score_ref[n] - peak) * (SCALE * LOG2E))
            total = total + (weights[:, :HD] + weights[:, HD:])
            mixed = mixed + jnp.dot(
                weights.astype(jnp.bfloat16), piece[1], preferred_element_type=jnp.float32
            )
        total = jnp.sum(total, axis=1, keepdims=True)
        out_ref[pl.ds(start, block), :] = (mixed / total).astype(jnp.bfloat16)
        lse = peak * SCALE + jnp.log(total)
        high = lse.astype(jnp.bfloat16).astype(jnp.float32)
        rest = lse - high
        middle = rest.astype(jnp.bfloat16).astype(jnp.float32)
        low = rest - middle
        lane = lax.broadcasted_iota(jnp.int32, (block, HD), 1)
        row = lax.broadcasted_iota(jnp.int32, (block, HD), 0) & 7
        stat = jnp.where(
            lane == row,
            high,
            jnp.where(lane == row + 8, middle, jnp.where(lane == row + 16, low, 0.0)),
        )
        stat = jnp.sum(stat.reshape(block // 8, 8, HD), axis=1)
        stat_ref[pl.ds(pl.multiple_of(index * (block // 8), block // 8), block // 8), :] = stat.astype(
            jnp.bfloat16
        )


def merge_kernel(prompt_ref, back_ref, near_ref, near_lse_ref, out_ref):
    slots = slots_of(prompt_ref)
    count = HEADS * HELD
    row = lax.broadcasted_iota(jnp.int32, (count, 1), 0)
    slot = spread(slots, row & 7)
    head = row >> 3
    lane = lax.broadcasted_iota(jnp.int32, (1, ROWS), 1)
    source = (lane >> 1) & 255
    inner = (lane >> 9) * 2 + (lane & 1)
    lane_key = ((source & 7) * 4 + (inner & 3)) * 64 + (source >> 3) * 2 + (inner >> 2)
    select = (head * 64 + slot == lane_key).astype(jnp.float32).astype(jnp.bfloat16)
    far = jnp.dot(select, back_ref[:ROWS, :], preferred_element_type=jnp.float32)
    stat_lane = lax.broadcasted_iota(jnp.int32, (1, 2 * DEVICES), 1)
    stat_select = (((slot >> 1) * 8 + (head >> 2)) * 2 == stat_lane).astype(jnp.float32).astype(jnp.bfloat16)
    stat = jnp.dot(stat_select, back_ref[ROWS:, :], preferred_element_type=jnp.float32)
    wide = lax.broadcasted_iota(jnp.int32, (count, HD), 1)
    mine = ((wide & 7) == (slot & 1) * 4 + (head & 3)) & (wide < 24)
    far_lse = jnp.sum(jnp.where(mine, stat, 0.0), axis=1, keepdims=True)
    near_lse = near_lse_ref[...].reshape(count, HD)
    top = jnp.maximum(far_lse, near_lse)
    far_scale = jnp.exp(far_lse - top)
    near_scale = jnp.exp(near_lse - top)
    merged = (far * far_scale + near_ref[...].reshape(count, HD) * near_scale) / (far_scale + near_scale)
    for h in range(HEADS):
        out_ref[:, h * HD : (h + 1) * HD] = merged[h * HELD : (h + 1) * HELD].astype(jnp.bfloat16)


VMEM = pl.BlockSpec(memory_space=pltpu.VMEM)
SMEM = pl.BlockSpec(memory_space=pltpu.SMEM)


def params(mib):
    return pltpu.CompilerParams(vmem_limit_bytes=mib << 20)


def shards(
    prompt_of,
    suffix_len,
    query,
    new_key,
    new_value,
    suffix_key,
    suffix_value,
    prefix_key,
    prefix_value,
):
    place = lax.axis_index(NEAR).astype(jnp.int32).reshape(1)
    cuts = pl.pallas_call(
        cut_kernel,
        out_shape=[jax.ShapeDtypeStruct((2, PIECE, HD), jnp.bfloat16)] * 8,
        in_specs=[SMEM, VMEM, VMEM],
        out_specs=[VMEM] * 8,
        compiler_params=params(16),
        name="cut",
    )(place, prefix_key, prefix_value)
    outgoing = pl.pallas_call(
        pack_kernel,
        out_shape=jax.ShapeDtypeStruct((ROWS, HD), jnp.bfloat16),
        in_specs=[SMEM, VMEM],
        out_specs=VMEM,
        compiler_params=params(16),
        name="pack",
    )(prompt_of, query)
    arrived = lax.all_to_all(outgoing.reshape(DEVICES, 8, HD), ALL, 0, 0, tiled=True)
    held = [cuts[0]]
    for step in range(1, 8):
        held.append(lax.ppermute(cuts[step], NEAR, [(i, i ^ step) for i in range(8)]))
    swapped = [lax.ppermute(piece, "c", [(0, 1), (1, 0)]) for piece in held]

    near_out, near_lse = pl.pallas_call(
        near_kernel,
        grid=(HELD,),
        out_shape=[jax.ShapeDtypeStruct((HEADS, HELD, HD), jnp.float32)] * 2,
        in_specs=[
            SMEM,
            pl.BlockSpec((1, HEADS, HD), lambda i: (i, 0, 0)),
            pl.BlockSpec((HELD, KVH * HD), lambda i: (0, 0)),
            pl.BlockSpec((HELD, KVH * HD), lambda i: (0, 0)),
            pl.BlockSpec((1, SUF, KVH * HD), lambda i: (i, 0, 0)),
            pl.BlockSpec((1, SUF, KVH * HD), lambda i: (i, 0, 0)),
        ],
        out_specs=[pl.BlockSpec((HEADS, HELD, HD), lambda i: (0, 0, 0))] * 2,
        compiler_params=params(16),
        cost_estimate=pl.CostEstimate(flops=300_000_000, bytes_accessed=4_500_000, transcendentals=65536),
        name="near",
    )(
        suffix_len,
        query.reshape(HELD, HEADS, HD),
        new_key.astype(jnp.float32),
        new_value.astype(jnp.float32),
        suffix_key,
        suffix_value,
    )

    far_out, far_stat = pl.pallas_call(
        far_kernel,
        out_shape=[
            jax.ShapeDtypeStruct((ROWS, HD), jnp.bfloat16),
            jax.ShapeDtypeStruct((DEVICES, HD), jnp.bfloat16),
        ],
        in_specs=[VMEM] * 17,
        out_specs=[VMEM] * 2,
        scratch_shapes=[pltpu.VMEM((16, 256, PIECE), jnp.float32)],
        compiler_params=params(32),
        name="far",
    )(arrived.reshape(ROWS, HD), *held, *swapped)
    parcel = jnp.concatenate(
        [
            far_out.reshape(DEVICES, 4, 2, HD),
            jnp.broadcast_to(far_stat.reshape(DEVICES, 1, 1, HD), (DEVICES, 1, 2, HD)),
        ],
        axis=1,
    )
    back = lax.all_to_all(parcel, ALL, 0, 0, tiled=True)
    back = back.transpose(1, 0, 2, 3).reshape(10 * DEVICES, HD)
    return pl.pallas_call(
        merge_kernel,
        out_shape=jax.ShapeDtypeStruct((HELD, HEADS * HD), jnp.bfloat16),
        in_specs=[SMEM, VMEM, VMEM, VMEM],
        out_specs=VMEM,
        compiler_params=params(16),
        name="merge",
    )(prompt_of, back, near_out, near_lse)


def solution(mesh):
    fine = Mesh(mesh.devices.reshape(2, 8, 2, 4, 2), ALL)
    grp = ("xh", "z")
    blk = ("xl", "y", "c")
    in_specs = (
        P(ALL),
        P(ALL),
        P(ALL, None),
        P(ALL, None),
        P(ALL, None),
        P(ALL, None, None),
        P(ALL, None, None),
        P(grp, blk, None),
        P(grp, blk, None),
    )
    return jax.shard_map(
        shards, mesh=fine, in_specs=in_specs, out_specs=P(ALL, None), check_vma=False
    )
```

time: 442 us -> 101 us (0.23)
  waiting for transfers between devices: 254 us -> 28.8 us
  local copies, waits for them, and re-layouts: 57.9 us -> 5.72 us
  matrix products: 41.1 us -> 0 us
  blocking collectives: 34.1 us -> 0 us
  Pallas kernels: 0 us -> 23.7 us
  between operations: 14 us -> 0.2 us
  starting transfers between devices: 33.7 us -> 39.3 us
    reduce_scatter x2 -> x0, waiting for transfers between devices: 111 us -> none  [the longest x1 68.6 us: shards(): lax.psum_scatter(local_out.reshape(total_rows, row_width), 'blk', scatter...]
    pmax x1 -> x0, waiting for transfers between devices: 108 us -> none  [shards(): global_max = lax.pmax(local_max, 'blk')]
    dot_general x16 -> x0, matrix products: 41.1 us -> none  [the longest x8 23.2 us: masked_scores(): jnp.einsum('rkgd,tkd->rkgt', heads_view, key_heads, preferred_element_typ...]
    dynamic_update_slice x16 -> x0, local copies, waits for them, and re-layouts: 24.5 us -> none  [the longest x8 24.1 us: shards(): lax.map(block_sums, (query_blocks, tag_blocks, global_max.reshape(-1, blo...]
    pallas_call x0 -> x5, Pallas kernels: none -> 23.7 us  [the longest x1 15.6 us: shards(): pl.pallas_call(far_kernel, out_shape=[jax.ShapeDtypeStruct((ROWS, HD), jn...]
    all_to_all x1 -> x0, blocking collectives: 22.4 us -> none  [shards(): lax.all_to_all(outgoing.reshape(groups, CAP, row_width), 'grp', split_axi...]
    ppermute x0 -> x15, starting transfers between devices: none -> 13.8 us  [the longest x7 12.3 us: shards(): lax.ppermute(cuts[step], NEAR, [(i, i ^ step) for i in range(8)])]
    dynamic_slice x14 -> x0, local copies, waits for them, and re-layouts: 12 us -> none  [the longest x8 10.4 us: shards(): lax.map(block_peak, (query_blocks, tag_blocks))]
  transfers between devices with their start and end apart: 8 -> 17, of which waited for: 7 -> 10; matrix products, arithmetic and copies ran while one was open for 3% -> 0% of each run, Pallas kernels for 0% -> 4%
where the time goes in v1:
time: 101 us; the launch traced here: 99.4 us
  starting transfers between devices  39.3 us (39%)
  waiting for transfers between devices  28.8 us (29%)
  Pallas kernels  23.7 us (23%)
  local copies, waits for them, and re-layouts  5.72 us (6%)
  other arithmetic  1.73 us (2%)
    all_to_all x1, waiting for transfers between devices, shards(): back = lax.all_to_all(parcel, ALL, 0, 0, tiled=True)  16.9 us
    pallas_call x1, Pallas kernels, shards(): pl.pallas_call(far_kernel, out_shape=[jax.ShapeDtypeStruct((ROWS, HD), jn...  15.6 us
    all_to_all x1, starting transfers between devices, shards(): lax.all_to_all(outgoing.reshape(DEVICES, 8, HD), ALL, 0, 0, tiled=True)  14.4 us
    ppermute x7, starting transfers between devices, shards(): lax.ppermute(cuts[step], NEAR, [(i, i ^ step) for i in range(8)])  12.3 us
    all_to_all x1, starting transfers between devices, shards(): back = lax.all_to_all(parcel, ALL, 0, 0, tiled=True)  11.1 us
    ppermute x7, waiting for transfers between devices, shards(): lax.ppermute(cuts[step], NEAR, [(i, i ^ step) for i in range(8)])  10.7 us
    unnamed x23, local copies, waits for them, and re-layouts  5.2 us
    pallas_call x1, Pallas kernels, shards(): pl.pallas_call(near_kernel, grid=(HELD,), out_shape=[jax.ShapeDtypeStruct...  4 us
  transfers between devices with their start and end apart: 17, of which 10 were waited for; matrix products, arithmetic and copies ran while one was open for 0% of the time, Pallas kernels for 4%

profile of v1, /device:TPU:32, one launch (start us, length us, event | category | flops | bytes accessed | tf_op | source)
XLA Modules:
  0.0 99.4 jit_solution(7724713746600014172)
XLA Ops:
  0.0 0.8 copy-done.4
  0.8 0.7 copy-done.6
  1.5 2.0 %pack.1 = bf16[2048,128]{1,0:T(8,128)(2,1)} custom-call(s32[8]{0:T(128)S(1)} %copy-done.6, bf16[8,4096]{1,0:T(8,128)(2,1)S(1)} %copy-done.4), custom_call_target="tpu_custom_call" | custom-call | tf_op jit(solution)/shard_map/pack/pallas_call | solution.py:225
  3.5 14.4 %all-to-all-start = ((bf16[256,8,128]{2,1,0:T(8,128)(2,1)}), bf16[256,8,128]{2,1,0:T(8,128)(2,1)S(1)}, u32[]{:S(2)}, u32[]{:S(2)}) async-start(bf16[256,8,128]{2,1,0:T(8,128)(2,1)} %bitcast), calls=%async_computation | async-start | bytes 1048576 | tf_op jit(solution)/shard_map/all_to_all | solution.py:233
  17.9 1.0 %copy-done.2 = bf16[2,256,512]{2,1,0:T(8,128)(2,1)S(1)} copy-done((bf16[2,256,512]{2,1,0:T(8,128)(2,1)S(1)}, bf16[2,256,512]{2,1,0:T(8,128)(2,1)}, u32[]{:S(2)}) %copy-start.2) | copy-done | bytes 524312
  19.0 1.0 %copy-done.3 = bf16[2,256,512]{2,1,0:T(8,128)(2,1)S(1)} copy-done((bf16[2,256,512]{2,1,0:T(8,128)(2,1)S(1)}, bf16[2,256,512]{2,1,0:T(8,128)(2,1)}, u32[]{:S(2)}) %copy-start.3) | copy-done | bytes 524312
  20.0 0.2 cut.1
  20.2 3.0 %collective-permute-start.2 = (bf16[2,256,128]{2,1,0:T(8,128)(2,1)S(1)}, bf16[2,256,128]{2,1,0:T(8,128)(2,1)S(1)}, u32[]{:S(2)}, u32[]{:S(2)}) collective-permute-start(bf16[2,256,128]{2,1,0:T(8,128)(2,1)S(1)} %get-tuple-element.20), channel_id=1, source_target_pairs={{0,6},{2,4},{4,2},{6,0},{8,14},{10,12},{12,10},{14,8},{1,7},{3,5},... | collective-permute-start | bytes 393224 | tf_op jit(solution)/shard_map/ppermute | solution.py:236
  23.2 1.5 %collective-permute-start.3 = (bf16[2,256,128]{2,1,0:T(8,128)(2,1)S(1)}, bf16[2,256,128]{2,1,0:T(8,128)(2,1)S(1)}, u32[]{:S(2)}, u32[]{:S(2)}) collective-permute-start(bf16[2,256,128]{2,1,0:T(8,128)(2,1)S(1)} %get-tuple-element.21), channel_id=1, source_target_pairs={{0,8},{2,10},{4,12},{6,14},{8,0},{10,2},{12,4},{14,6},{1,9},{3,11}... | collective-permute-start | bytes 393224 | tf_op jit(solution)/shard_map/ppermute | solution.py:236
  24.8 2.6 %collective-permute-start.5 = (bf16[2,256,128]{2,1,0:T(8,128)(2,1)S(1)}, bf16[2,256,128]{2,1,0:T(8,128)(2,1)S(1)}, u32[]{:S(2)}, u32[]{:S(2)}) collective-permute-start(bf16[2,256,128]{2,1,0:T(8,128)(2,1)S(1)} %get-tuple-element.23), channel_id=1, source_target_pairs={{0,12},{2,14},{4,8},{6,10},{8,4},{10,6},{12,0},{14,2},{1,13},{3,15... | collective-permute-start | bytes 393224 | tf_op jit(solution)/shard_map/ppermute | solution.py:236
  27.4 2.9 %collective-permute-start.6 = (bf16[2,256,128]{2,1,0:T(8,128)(2,1)S(1)}, bf16[2,256,128]{2,1,0:T(8,128)(2,1)S(1)}, u32[]{:S(2)}, u32[]{:S(2)}) collective-permute-start(bf16[2,256,128]{2,1,0:T(8,128)(2,1)S(1)} %get-tuple-element.24), channel_id=1, source_target_pairs={{0,14},{2,12},{4,10},{6,8},{8,6},{10,4},{12,2},{14,0},{1,15},{3,13... | collective-permute-start | bytes 393224 | tf_op jit(solution)/shard_map/ppermute | solution.py:236
  30.2 0.8 collective-permute-done.3.refs_4_
  31.1 2.3 %collective-permute-start.1 = (bf16[2,256,128]{2,1,0:T(8,128)(2,1)S(1)}, bf16[2,256,128]{2,1,0:T(8,128)(2,1)S(1)}, u32[]{:S(2)}, u32[]{:S(2)}) collective-permute-start(bf16[2,256,128]{2,1,0:T(8,128)(2,1)S(1)} %get-tuple-element.19), channel_id=1, source_target_pairs={{0,4},{2,6},{4,0},{6,2},{8,12},{10,14},{12,8},{14,10},{1,5},{3,7},... | collective-permute-start | bytes 393224 | tf_op jit(solution)/shard_map/ppermute | solution.py:236
  33.3 1.3 %collective-permute-done.4.refs_5_ = bf16[2,256,128]{2,1,0:T(8,128)(2,1)S(1)} collective-permute-done((bf16[2,256,128]{2,1,0:T(8,128)(2,1)S(1)}, bf16[2,256,128]{2,1,0:T(8,128)(2,1)S(1)}, u32[]{:S(2)}, u32[]{:S(2)}) %collective-permute-start.4) | collective-permute-done | bytes 131104 | tf_op jit(solution)/shard_map/ppermute | solution.py:236
  34.6 4.5 %collective-permute-done.5.refs_6_ = bf16[2,256,128]{2,1,0:T(8,128)(2,1)S(1)} collective-permute-done((bf16[2,256,128]{2,1,0:T(8,128)(2,1)S(1)}, bf16[2,256,128]{2,1,0:T(8,128)(2,1)S(1)}, u32[]{:S(2)}, u32[]{:S(2)}) %collective-permute-start.5) | collective-permute-done | bytes 131104 | tf_op jit(solution)/shard_map/ppermute | solution.py:236
  39.1 1.9 %collective-permute-done.6.refs_7_ = bf16[2,256,128]{2,1,0:T(8,128)(2,1)S(1)} collective-permute-done((bf16[2,256,128]{2,1,0:T(8,128)(2,1)S(1)}, bf16[2,256,128]{2,1,0:T(8,128)(2,1)S(1)}, u32[]{:S(2)}, u32[]{:S(2)}) %collective-permute-start.6) | collective-permute-done | bytes 131104 | tf_op jit(solution)/shard_map/ppermute | solution.py:236
  41.0 0.5 collective-permute-start.12
  41.5 2.2 %collective-permute-done.1.refs_2_ = bf16[2,256,128]{2,1,0:T(8,128)(2,1)S(1)} collective-permute-done((bf16[2,256,128]{2,1,0:T(8,128)(2,1)S(1)}, bf16[2,256,128]{2,1,0:T(8,128)(2,1)S(1)}, u32[]{:S(2)}, u32[]{:S(2)}) %collective-permute-start.1) | collective-permute-done | bytes 131104 | tf_op jit(solution)/shard_map/ppermute | solution.py:236
  43.7 0.5 collective-permute-start.14
  44.4 0.4 collective-permute-start.9
  44.8 0.3 collective-permute-done.13.refs_14_
  45.1 0.2 collective-permute-done.14.refs_15_
  45.3 0.3 collective-permute-done.8.refs_9_
  45.6 0.3 collective-permute-done.9.refs_10_
  45.9 15.6 %far.1 = (bf16[2048,128]{1,0:T(8,128)(2,1)S(1)}, bf16[256,128]{1,0:T(8,128)(2,1)S(1)}) custom-call(bf16[2048,128]{1,0:T(8,128)(2,1)S(1)} %bitcast.11, bf16[2,256,128]{2,1,0:T(8,128)(2,1)S(1)} %get-tuple-element.17.refs_0_, bf16[2,256,128]{2,1,0:T(8,128)(2,1)S(1)} %collective-permute-done.refs_1_, bf16[2,256,128]{2,1,0:T(8,128)(2,1)S(1)} %collective-permute-done.1.refs_2_, ...), custom_call_target="tpu_custom_call" | custom-call | tf_op jit(solution)/shard_map/far/pallas_call | solution.py:264
  61.6 1.7 %pad_maximum_fusion = bf16[256,5,2,128]{3,2,1,0:T(2,128)(2,1)} fusion(bf16[256,1,2,128]{3,2,1,0:T(2,128)(2,1)S(1)} %broadcast_in_dim.2, bf16[256,4,2,128]{3,2,1,0:T(2,128)(2,1)S(1)} %bitcast.12), kind=kLoop, calls=%fused_computation | loop fusion | flops 327680 | bytes 1310720 | tf_op jit(solution)/shard_map/concatenate | solution.py:276
  63.4 11.1 %all-to-all-start.1 = ((bf16[256,5,2,128]{3,2,1,0:T(2,128)(2,1)}), bf16[256,5,2,128]{3,2,1,0:T(2,128)(2,1)S(1)}, u32[]{:S(2)}, u32[]{:S(2)}) async-start(bf16[256,5,2,128]{3,2,1,0:T(2,128)(2,1)} %pad_maximum_fusion), calls=%async_computation.1 | async-start | bytes 1310720 | tf_op jit(solution)/shard_map/all_to_all | solution.py:283
  74.6 1.6 %copy-done.1 = bf16[8,256,512]{2,1,0:T(8,128)(2,1)S(1)} copy-done((bf16[8,256,512]{2,1,0:T(8,128)(2,1)S(1)}, bf16[8,256,512]{2,1,0:T(8,128)(2,1)}, u32[]{:S(2)}) %copy-start.1) | copy-done | bytes 2097176
  76.2 4.0 %near.1 = (f32[32,8,128]{2,1,0:T(8,128)S(1)}, f32[32,8,128]{2,1,0:T(8,128)S(1)}) custom-call(s32[8]{0:T(128)S(1)} %copy-done.8, bf16[8,32,128]{2,1,0:T(8,128)(2,1)S(1)} %bitcast.13, f32[8,512]{1,0:T(8,128)S(1)} %convert_element_type.6.new_key_ref, f32[8,512]{1,0:T(8,128)S(1)} %convert_element_type.7.new_value_ref, bf16[8,256,512]{2,1,0:T(8,128)(2,1)S(1)} %copy-done, ...), custom_call_target="tpu_custom_call" | custom-call | flops 300000000 | bytes 4500000 | tf_op jit(solution)/shard_map/near/pallas_call | solution.py:239
  80.2 16.9 %all-to-all-done.1 = bf16[256,5,2,128]{3,2,1,0:T(2,128)(2,1)S(1)} async-done(((bf16[256,5,2,128]{3,2,1,0:T(2,128)(2,1)}), bf16[256,5,2,128]{3,2,1,0:T(2,128)(2,1)S(1)}, u32[]{:S(2)}, u32[]{:S(2)}) %all-to-all-start.1) | async-done | bytes 655392 | tf_op jit(solution)/shard_map/all_to_all | solution.py:283
  97.1 0.5 copy.11
  97.6 1.8 %merge.1 = bf16[8,4096]{1,0:T(8,128)(2,1)} custom-call(s32[8]{0:T(128)S(1)} %copy-done.7, bf16[2560,128]{1,0:T(8,128)(2,1)S(1)} %bitcast.10, f32[32,8,128]{2,1,0:T(8,128)S(1)} %get-tuple-element.27.near_ref, f32[32,8,128]{2,1,0:T(8,128)S(1)} %get-tuple-element.28.near_lse_ref), custom_call_target="tpu_custom_call" | custom-call | tf_op jit(solution)/shard_map/merge/pallas_call | solution.py:285
  (35 shorter events, 0.4 us)
Async XLA Ops:
  0.0 0.8 copy-start.4
  0.8 0.7 copy-start.6
  3.5 42.4 %all-to-all-start = ((bf16[256,8,128]{2,1,0:T(8,128)(2,1)}), bf16[256,8,128]{2,1,0:T(8,128)(2,1)S(1)}, u32[]{:S(2)}, u32[]{:S(2)}) async-start(bf16[256,8,128]{2,1,0:T(8,128)(2,1)} %bitcast), calls=%async_computation | async-start | bytes 1048576 | tf_op jit(solution)/shard_map/all_to_all | solution.py:233
  17.9 1.0 %copy-start.2 = (bf16[2,256,512]{2,1,0:T(8,128)(2,1)S(1)}, bf16[2,256,512]{2,1,0:T(8,128)(2,1)}, u32[]{:S(2)}) copy-start(bf16[2,256,512]{2,1,0:T(8,128)(2,1)} %key_ref.2) | copy-start | bytes 1572868
  19.0 1.0 %copy-start.3 = (bf16[2,256,512]{2,1,0:T(8,128)(2,1)S(1)}, bf16[2,256,512]{2,1,0:T(8,128)(2,1)}, u32[]{:S(2)}) copy-start(bf16[2,256,512]{2,1,0:T(8,128)(2,1)} %value_ref.2) | copy-start | bytes 1572868
  20.2 10.0 %collective-permute-start.2 = (bf16[2,256,128]{2,1,0:T(8,128)(2,1)S(1)}, bf16[2,256,128]{2,1,0:T(8,128)(2,1)S(1)}, u32[]{:S(2)}, u32[]{:S(2)}) collective-permute-start(bf16[2,256,128]{2,1,0:T(8,128)(2,1)S(1)} %get-tuple-element.20), channel_id=1, source_target_pairs={{0,6},{2,4},{4,2},{6,0},{8,14},{10,12},{12,10},{14,8},{1,7},{3,5},... | collective-permute-start | bytes 393224 | tf_op jit(solution)/shard_map/ppermute | solution.py:236
  23.2 7.9 %collective-permute-start.3 = (bf16[2,256,128]{2,1,0:T(8,128)(2,1)S(1)}, bf16[2,256,128]{2,1,0:T(8,128)(2,1)S(1)}, u32[]{:S(2)}, u32[]{:S(2)}) collective-permute-start(bf16[2,256,128]{2,1,0:T(8,128)(2,1)S(1)} %get-tuple-element.21), channel_id=1, source_target_pairs={{0,8},{2,10},{4,12},{6,14},{8,0},{10,2},{12,4},{14,6},{1,9},{3,11}... | collective-permute-start | bytes 393224 | tf_op jit(solution)/shard_map/ppermute | solution.py:236
  24.6 10.0 %collective-permute-start.4 = (bf16[2,256,128]{2,1,0:T(8,128)(2,1)S(1)}, bf16[2,256,128]{2,1,0:T(8,128)(2,1)S(1)}, u32[]{:S(2)}, u32[]{:S(2)}) collective-permute-start(bf16[2,256,128]{2,1,0:T(8,128)(2,1)S(1)} %get-tuple-element.22), channel_id=1, source_target_pairs={{0,10},{2,8},{4,14},{6,12},{8,2},{10,0},{12,6},{14,4},{1,11},{3,9}... | collective-permute-start | bytes 393224 | tf_op jit(solution)/shard_map/ppermute | solution.py:236
  24.8 14.2 %collective-permute-start.5 = (bf16[2,256,128]{2,1,0:T(8,128)(2,1)S(1)}, bf16[2,256,128]{2,1,0:T(8,128)(2,1)S(1)}, u32[]{:S(2)}, u32[]{:S(2)}) collective-permute-start(bf16[2,256,128]{2,1,0:T(8,128)(2,1)S(1)} %get-tuple-element.23), channel_id=1, source_target_pairs={{0,12},{2,14},{4,8},{6,10},{8,4},{10,6},{12,0},{14,2},{1,13},{3,15... | collective-permute-start | bytes 393224 | tf_op jit(solution)/shard_map/ppermute | solution.py:236
  27.4 13.6 %collective-permute-start.6 = (bf16[2,256,128]{2,1,0:T(8,128)(2,1)S(1)}, bf16[2,256,128]{2,1,0:T(8,128)(2,1)S(1)}, u32[]{:S(2)}, u32[]{:S(2)}) collective-permute-start(bf16[2,256,128]{2,1,0:T(8,128)(2,1)S(1)} %get-tuple-element.24), channel_id=1, source_target_pairs={{0,14},{2,12},{4,10},{6,8},{8,6},{10,4},{12,2},{14,0},{1,15},{3,13... | collective-permute-start | bytes 393224 | tf_op jit(solution)/shard_map/ppermute | solution.py:236
  30.2 10.8 %collective-permute-start = (bf16[2,256,128]{2,1,0:T(8,128)(2,1)S(1)}, bf16[2,256,128]{2,1,0:T(8,128)(2,1)S(1)}, u32[]{:S(2)}, u32[]{:S(2)}) collective-permute-start(bf16[2,256,128]{2,1,0:T(8,128)(2,1)S(1)} %get-tuple-element.18), channel_id=1, source_target_pairs={{0,2},{2,0},{4,6},{6,4},{8,10},{10,8},{12,14},{14,12},{1,3},{3,1},... | collective-permute-start | bytes 393224 | tf_op jit(solution)/shard_map/ppermute | solution.py:236
  31.1 12.7 %collective-permute-start.1 = (bf16[2,256,128]{2,1,0:T(8,128)(2,1)S(1)}, bf16[2,256,128]{2,1,0:T(8,128)(2,1)S(1)}, u32[]{:S(2)}, u32[]{:S(2)}) collective-permute-start(bf16[2,256,128]{2,1,0:T(8,128)(2,1)S(1)} %get-tuple-element.19), channel_id=1, source_target_pairs={{0,4},{2,6},{4,0},{6,2},{8,12},{10,14},{12,8},{14,10},{1,5},{3,7},... | collective-permute-start | bytes 393224 | tf_op jit(solution)/shard_map/ppermute | solution.py:236
  34.6 9.1 %collective-permute-start.7 = (bf16[2,256,128]{2,1,0:T(8,128)(2,1)S(1)}, bf16[2,256,128]{2,1,0:T(8,128)(2,1)S(1)}, u32[]{:S(2)}, u32[]{:S(2)}) collective-permute-start(bf16[2,256,128]{2,1,0:T(8,128)(2,1)S(1)} %get-tuple-element.17.refs_0_), channel_id=1, source_target_pairs={{0,1},{1,0},{2,3},{3,2},{4,5},{5,4},{6,7},{7,6},{8,9},{9,8},{10,11... | collective-permute-start | bytes 393224 | tf_op jit(solution)/shard_map/ppermute | solution.py:237
  39.1 5.2 %collective-permute-start.10 = (bf16[2,256,128]{2,1,0:T(8,128)(2,1)S(1)}, bf16[2,256,128]{2,1,0:T(8,128)(2,1)S(1)}, u32[]{:S(2)}, u32[]{:S(2)}) collective-permute-start(bf16[2,256,128]{2,1,0:T(8,128)(2,1)S(1)} %collective-permute-done.2.refs_3_), channel_id=1, source_target_pairs={{0,1},{1,0},{2,3},{3,2},{4,5},{5,4},{6,7},{7,6},{8,9},{9,8},{10,11... | collective-permute-start | bytes 393224 | tf_op jit(solution)/shard_map/ppermute | solution.py:237
  41.0 3.4 %collective-permute-start.11 = (bf16[2,256,128]{2,1,0:T(8,128)(2,1)S(1)}, bf16[2,256,128]{2,1,0:T(8,128)(2,1)S(1)}, u32[]{:S(2)}, u32[]{:S(2)}) collective-permute-start(bf16[2,256,128]{2,1,0:T(8,128)(2,1)S(1)} %collective-permute-done.3.refs_4_), channel_id=1, source_target_pairs={{0,1},{1,0},{2,3},{3,2},{4,5},{5,4},{6,7},{7,6},{8,9},{9,8},{10,11... | collective-permute-start | bytes 393224 | tf_op jit(solution)/shard_map/ppermute | solution.py:237
  41.0 3.8 %collective-permute-start.12 = (bf16[2,256,128]{2,1,0:T(8,128)(2,1)S(1)}, bf16[2,256,128]{2,1,0:T(8,128)(2,1)S(1)}, u32[]{:S(2)}, u32[]{:S(2)}) collective-permute-start(bf16[2,256,128]{2,1,0:T(8,128)(2,1)S(1)} %collective-permute-done.4.refs_5_), channel_id=1, source_target_pairs={{0,1},{1,0},{2,3},{3,2},{4,5},{5,4},{6,7},{7,6},{8,9},{9,8},{10,11... | collective-permute-start | bytes 393224 | tf_op jit(solution)/shard_map/ppermute | solution.py:237
  43.7 1.3 %collective-permute-start.13 = (bf16[2,256,128]{2,1,0:T(8,128)(2,1)S(1)}, bf16[2,256,128]{2,1,0:T(8,128)(2,1)S(1)}, u32[]{:S(2)}, u32[]{:S(2)}) collective-permute-start(bf16[2,256,128]{2,1,0:T(8,128)(2,1)S(1)} %collective-permute-done.5.refs_6_), channel_id=1, source_target_pairs={{0,1},{1,0},{2,3},{3,2},{4,5},{5,4},{6,7},{7,6},{8,9},{9,8},{10,11... | collective-permute-start | bytes 393224 | tf_op jit(solution)/shard_map/ppermute | solution.py:237
  43.7 1.5 %collective-permute-start.14 = (bf16[2,256,128]{2,1,0:T(8,128)(2,1)S(1)}, bf16[2,256,128]{2,1,0:T(8,128)(2,1)S(1)}, u32[]{:S(2)}, u32[]{:S(2)}) collective-permute-start(bf16[2,256,128]{2,1,0:T(8,128)(2,1)S(1)} %collective-permute-done.6.refs_7_), channel_id=1, source_target_pairs={{0,1},{1,0},{2,3},{3,2},{4,5},{5,4},{6,7},{7,6},{8,9},{9,8},{10,11... | collective-permute-start | bytes 393224 | tf_op jit(solution)/shard_map/ppermute | solution.py:237
  44.3 1.3 %collective-permute-start.8 = (bf16[2,256,128]{2,1,0:T(8,128)(2,1)S(1)}, bf16[2,256,128]{2,1,0:T(8,128)(2,1)S(1)}, u32[]{:S(2)}, u32[]{:S(2)}) collective-permute-start(bf16[2,256,128]{2,1,0:T(8,128)(2,1)S(1)} %collective-permute-done.refs_1_), channel_id=1, source_target_pairs={{0,1},{1,0},{2,3},{3,2},{4,5},{5,4},{6,7},{7,6},{8,9},{9,8},{10,11... | collective-permute-start | bytes 393224 | tf_op jit(solution)/shard_map/ppermute | solution.py:237
  44.4 1.5 %collective-permute-start.9 = (bf16[2,256,128]{2,1,0:T(8,128)(2,1)S(1)}, bf16[2,256,128]{2,1,0:T(8,128)(2,1)S(1)}, u32[]{:S(2)}, u32[]{:S(2)}) collective-permute-start(bf16[2,256,128]{2,1,0:T(8,128)(2,1)S(1)} %collective-permute-done.1.refs_2_), channel_id=1, source_target_pairs={{0,1},{1,0},{2,3},{3,2},{4,5},{5,4},{6,7},{7,6},{8,9},{9,8},{10,11... | collective-permute-start | bytes 393224 | tf_op jit(solution)/shard_map/ppermute | solution.py:237
  45.9 28.6 %copy-start.5 = (bf16[8,4096]{1,0:T(8,128)(2,1)S(1)}, bf16[8,4096]{1,0:T(8,128)(2,1)}, u32[]{:S(2)}) copy-start(bf16[8,4096]{1,0:T(8,128)(2,1)} %query_ref.1) | copy-start | bytes 196612
  61.5 13.0 %copy-start.9 = (bf16[8,512]{1,0:T(8,128)(2,1)S(1)}, bf16[8,512]{1,0:T(8,128)(2,1)}, u32[]{:S(2)}) copy-start(bf16[8,512]{1,0:T(8,128)(2,1)} %param.12) | copy-start | bytes 24580
  61.5 13.0 %copy-start.10 = (bf16[8,512]{1,0:T(8,128)(2,1)S(1)}, bf16[8,512]{1,0:T(8,128)(2,1)}, u32[]{:S(2)}) copy-start(bf16[8,512]{1,0:T(8,128)(2,1)} %param.13) | copy-start | bytes 24580
  61.5 13.0 %copy-start = (bf16[8,256,512]{2,1,0:T(8,128)(2,1)S(1)}, bf16[8,256,512]{2,1,0:T(8,128)(2,1)}, u32[]{:S(2)}) copy-start(bf16[8,256,512]{2,1,0:T(8,128)(2,1)} %key_ref.3) | copy-start | bytes 6291460
  61.6 13.0 %copy-start.8 = (s32[8]{0:T(128)S(1)}, s32[8]{0:T(128)}, u32[]{:S(2)}) copy-start(s32[8]{0:T(128)} %len_ref.1) | copy-start | bytes 100
  63.4 33.7 %all-to-all-start.1 = ((bf16[256,5,2,128]{3,2,1,0:T(2,128)(2,1)}), bf16[256,5,2,128]{3,2,1,0:T(2,128)(2,1)S(1)}, u32[]{:S(2)}, u32[]{:S(2)}) async-start(bf16[256,5,2,128]{3,2,1,0:T(2,128)(2,1)} %pad_maximum_fusion), calls=%async_computation.1 | async-start | bytes 1310720 | tf_op jit(solution)/shard_map/all_to_all | solution.py:283
  74.6 1.6 %copy-start.1 = (bf16[8,256,512]{2,1,0:T(8,128)(2,1)S(1)}, bf16[8,256,512]{2,1,0:T(8,128)(2,1)}, u32[]{:S(2)}) copy-start(bf16[8,256,512]{2,1,0:T(8,128)(2,1)} %value_ref.3) | copy-start | bytes 6291460
  76.2 21.4 %copy-start.7 = (s32[8]{0:T(128)S(1)}, s32[8]{0:T(128)}, u32[]{:S(2)}) copy-start(s32[8]{0:T(128)} %prompt_ref.3) | copy-start | bytes 100

commit v2 on v1

v2 whole, which is shorter than its diff:
```python
import math

import jax
import jax.numpy as jnp
from jax import lax
from jax.experimental import pallas as pl
from jax.experimental.pallas import tpu as pltpu
from jax.sharding import Mesh, PartitionSpec as P

HD = 128
CAP = 2
HELD = 8
HEADS = 32
KVH = 4
RATIO = 8
PROMPTS = 32
SUF = 256
PIECE = 256
SLOTS = 256
ROWS = SLOTS * RATIO
NEG = -1e30
SCALE = HD ** (-0.5)
LOG2E = 1.4426950408889634
ALL = ("xh", "z", "xl", "y", "c")
NEAR = ("xl", "y")
FAR = ("xh", "z", "xl")


def slots_of(prompt_ref):
    prompts = [prompt_ref[i] for i in range(HELD)]
    slots = []
    for i in range(HELD):
        rank = jnp.int32(0)
        for j in range(i):
            rank = rank + jnp.where(prompts[j] == prompts[i], 1, 0)
        slots.append(prompts[i] * CAP + rank)
    return slots


def spread(values, index):
    picked = jnp.zeros(index.shape, jnp.int32)
    for i, value in enumerate(values):
        picked = jnp.where(index == i, value, picked)
    return picked


def prep_kernel(place_ref, prompt_ref, query_ref, key_ref, value_ref, send_ref, *cut_refs):
    slots = slots_of(prompt_ref)
    lane = lax.broadcasted_iota(jnp.int32, (HELD, HD), 1)
    row = lax.broadcasted_iota(jnp.int32, (HELD, HD), 0)
    tags = jnp.concatenate(
        [spread(slots, lane & 7).astype(jnp.float32), spread(slots, row).astype(jnp.float32)], axis=0
    ).astype(jnp.bfloat16)
    for y in range(KVH):
        send_ref[y, :64] = jnp.concatenate(
            [
                query_ref[:, h * HD : (h + 1) * HD].astype(jnp.float32)
                for h in range(y * RATIO, (y + 1) * RATIO)
            ],
            axis=0,
        ).astype(jnp.bfloat16)
        send_ref[y, 64:] = tags
    place = place_ref[0]
    for step, cut_ref in enumerate(cut_refs):
        target = place ^ step
        prompt = target >> 2
        column = pl.multiple_of((target & 3) * HD, HD)
        cut_ref[0] = key_ref[prompt, :, pl.ds(column, HD)]
        cut_ref[1] = value_ref[prompt, :, pl.ds(column, HD)]


def pack_kernel(got_ref, out_ref):
    held = got_ref[:, :64].reshape(256, HD)
    tags = [got_ref[y, 64:].astype(jnp.float32)[:1].astype(jnp.int32) for y in range(KVH)]
    half = lax.broadcasted_iota(jnp.int32, (1, HD), 1) < 64
    tag = jnp.concatenate([jnp.where(half, tags[0], tags[1]), jnp.where(half, tags[2], tags[3])], axis=1)
    lane_key = (lax.broadcasted_iota(jnp.int32, (1, 256), 1) >> 3) * 64 + tag
    chunk = 512
    for start in range(0, ROWS, chunk):
        row = lax.broadcasted_iota(jnp.int32, (chunk, 1), 0) + start
        row_key = ((row >> 1) & 3) * 512 + ((row >> 3) & 7) * 64 + (row >> 6) * 2 + (row & 1)
        select = (row_key == lane_key).astype(jnp.float32).astype(jnp.bfloat16)
        out_ref[start : start + chunk, :] = jnp.dot(
            select, held, preferred_element_type=jnp.float32
        ).astype(jnp.bfloat16)


def near_kernel(len_ref, query_ref, new_key_ref, new_value_ref, key_ref, value_ref, out_ref, lse_ref):
    step = pl.program_id(0)
    length = len_ref[step]
    query = query_ref[0]
    keys = key_ref[0]
    values = value_ref[0]
    new_key = new_key_ref[pl.ds(step, 1), :]
    new_value = new_value_ref[pl.ds(step, 1), :]

    def spread_heads(row):
        return jnp.concatenate(
            [jnp.broadcast_to(row[:, k * HD : (k + 1) * HD], (RATIO, HD)) for k in range(KVH)], axis=0
        )

    scores = jnp.concatenate(
        [
            lax.dot_general(
                query,
                keys[:, k * HD : (k + 1) * HD],
                (((1,), (1,)), ((), ())),
                preferred_element_type=jnp.float32,
            )[k * RATIO : (k + 1) * RATIO]
            for k in range(KVH)
        ],
        axis=0,
    ) * SCALE
    own = jnp.sum(query.astype(jnp.float32) * spread_heads(new_key), axis=1, keepdims=True) * SCALE
    live = lax.broadcasted_iota(jnp.int32, (1, SUF), 1) < length
    scores = jnp.where(live, scores, NEG)
    top = jnp.maximum(jnp.max(scores, axis=1, keepdims=True), own)
    weights = jnp.where(live, jnp.exp(scores - top), 0.0)
    own_weight = jnp.exp(own - top)
    total = jnp.sum(weights, axis=1, keepdims=True) + own_weight
    rounded = weights.astype(jnp.bfloat16)
    mixed = jnp.concatenate(
        [
            jnp.dot(rounded, values[:, k * HD : (k + 1) * HD], preferred_element_type=jnp.float32)[
                k * RATIO : (k + 1) * RATIO
            ]
            for k in range(KVH)
        ],
        axis=0,
    )
    mixed = mixed + own_weight.astype(jnp.bfloat16).astype(jnp.float32) * spread_heads(new_value)
    out_ref[:, pl.ds(step, 1), :] = (mixed / total).reshape(HEADS, 1, HD)
    lse_ref[:, pl.ds(step, 1), :] = jnp.broadcast_to(top + jnp.log(total), (HEADS, HD)).reshape(
        HEADS, 1, HD
    )


def far_kernel(query_ref, *refs):
    pieces = refs[:16]
    out_ref, score_ref, query_scr, mixed_scr, stat_scr = refs[16:]
    span = 32
    block = span * RATIO
    tokens = 16 * PIECE
    queries = query_ref[...].astype(jnp.float32).reshape(32, RATIO, 8, HD)
    biggest = jnp.max(jnp.max(jnp.abs(queries), axis=1).reshape(SLOTS, HD), axis=1, keepdims=True)
    valid = (biggest > 0).astype(jnp.float32)
    row = lax.broadcasted_iota(jnp.int32, (SLOTS, SLOTS), 0)
    lane = lax.broadcasted_iota(jnp.int32, (SLOTS, SLOTS), 1)
    wide = jnp.broadcast_to(valid, (SLOTS, SLOTS)).astype(jnp.bfloat16)
    before = jnp.dot(
        (lane < row).astype(jnp.float32).astype(jnp.bfloat16), wide, preferred_element_type=jnp.float32
    )
    order = jnp.where(valid > 0, before, -1.0).astype(jnp.int32)
    gather = (order == lane).astype(jnp.float32).astype(jnp.bfloat16)
    count = jnp.sum(valid).astype(jnp.int32)
    for h in range(RATIO):
        query_scr[h] = lax.dot_general(
            gather,
            queries[:, h].reshape(SLOTS, HD).astype(jnp.bfloat16),
            (((0,), (0,)), ((), ())),
            preferred_element_type=jnp.float32,
        ).astype(jnp.bfloat16)
    mixed_scr[...] = jnp.zeros_like(mixed_scr)
    stat_scr[...] = jnp.zeros_like(stat_scr)

    @pl.loop(0, (count + span - 1) // span)
    def _(index):
        start = pl.multiple_of(index * span, span)
        query = query_scr[:, pl.ds(start, span), :].reshape(block, HD)
        peak = jnp.full((block, HD), -jnp.inf, jnp.float32)
        for n, piece in enumerate(pieces):
            scores = lax.dot_general(
                query, piece[0], (((1,), (1,)), ((), ())), preferred_element_type=jnp.float32
            )
            score_ref[n] = scores
            peak = jnp.maximum(peak, jnp.maximum(scores[:, :HD], scores[:, HD:]))
        peak = jnp.max(peak, axis=1, keepdims=True)
        total = jnp.zeros((block, HD), jnp.float32)
        mixed = jnp.zeros((block, HD), jnp.float32)
        for n, piece in enumerate(pieces):
            weights = jnp.exp2((score_ref[n] - peak) * (SCALE * LOG2E))
            total = total + (weights[:, :HD] + weights[:, HD:])
            mixed = mixed + jnp.dot(
                weights.astype(jnp.bfloat16), piece[1], preferred_element_type=jnp.float32
            )
        total = jnp.sum(total, axis=1, keepdims=True)
        mixed_scr[:, pl.ds(start, span), :] = (mixed / total).astype(jnp.bfloat16).reshape(RATIO, span, HD)
        lse = peak * SCALE + jnp.log(total)
        stat_scr[pl.ds(start, span), :] = split_stat(lse.reshape(RATIO, span, 1), span).astype(jnp.bfloat16)

    idle = 1.0 - valid
    mean = sum(piece[1].astype(jnp.float32).reshape(PIECE // 8, 8, HD).sum(axis=0) for piece in pieces)
    mean = jnp.sum(mean, axis=0, keepdims=True) / tokens
    heads = []
    for h in range(RATIO):
        spread_out = jnp.dot(gather, mixed_scr[h], preferred_element_type=jnp.float32) + idle * mean
        heads.append(spread_out.reshape(32, 8, HD))
    for h in range(0, RATIO, 2):
        out_ref[:, h * 8 : h * 8 + 16] = jnp.concatenate(heads[h : h + 2], axis=1).astype(jnp.bfloat16)
    even = split_stat(jnp.full((RATIO, SLOTS, 1), math.log(tokens), jnp.float32), SLOTS)
    stat = jnp.dot(gather, stat_scr[...], preferred_element_type=jnp.float32) + idle * even
    stat = stat.reshape(32, 8, HD)
    out_ref[:, 64:] = jnp.concatenate([stat, jnp.zeros_like(stat)], axis=1).astype(jnp.bfloat16)


def split_stat(lse, span):
    high = lse.astype(jnp.bfloat16).astype(jnp.float32)
    rest = lse - high
    middle = rest.astype(jnp.bfloat16).astype(jnp.float32)
    low = rest - middle
    lane = lax.broadcasted_iota(jnp.int32, (span, HD), 1)
    stat = jnp.zeros((span, HD), jnp.float32)
    for h in range(RATIO):
        for n, part in enumerate((high, middle, low)):
            stat = jnp.where(lane == n * 8 + h, part[h], stat)
    return stat


def select_kernel(got_ref, back_ref, send_ref):
    tags = [got_ref[y, 64:].astype(jnp.float32)[8:, :1].astype(jnp.int32) for y in range(KVH)]
    lane = lax.broadcasted_iota(jnp.int32, (1, ROWS), 1)
    lane_key = ((lane >> 1) & 3) * 512 + ((lane >> 3) & 7) * 64 + (lane >> 6) * 2 + (lane & 1)
    tag = jnp.concatenate([tags[y] for y in range(KVH) for _ in range(RATIO)], axis=0)
    row_key = (lax.broadcasted_iota(jnp.int32, (256, 1), 0) >> 3) * 64 + tag
    select = (row_key == lane_key).astype(jnp.float32).astype(jnp.bfloat16)
    far = jnp.dot(select, back_ref[:, :64].reshape(ROWS, HD), preferred_element_type=jnp.float32)
    send_ref[:, :64] = far.astype(jnp.bfloat16).reshape(KVH, 64, HD)
    stats = back_ref[:, 64:].astype(jnp.float32)[:, :8].reshape(SLOTS, HD).astype(jnp.bfloat16)
    lane = lax.broadcasted_iota(jnp.int32, (1, SLOTS), 1)
    lane_key = ((lane >> 1) & 3) * 64 + (lane >> 3) * 2 + (lane & 1)
    row_key = (lax.broadcasted_iota(jnp.int32, (32, 1), 0) >> 3) * 64 + jnp.concatenate(tags, axis=0)
    select = (row_key == lane_key).astype(jnp.float32).astype(jnp.bfloat16)
    stat = jnp.dot(select, stats, preferred_element_type=jnp.float32).reshape(KVH, 8, HD)
    send_ref[:, 64:] = jnp.concatenate([stat, jnp.zeros_like(stat)], axis=1).astype(jnp.bfloat16)


def merge_kernel(back_ref, near_ref, near_lse_ref, out_ref):
    lane = lax.broadcasted_iota(jnp.int32, (HELD, HD), 1)
    for y in range(KVH):
        far = back_ref[y, :64].astype(jnp.float32)
        stat = jnp.where(lane < 24, back_ref[y, 64:].astype(jnp.float32)[:8], 0.0)
        for h in range(RATIO):
            head = y * RATIO + h
            far_lse = jnp.sum(jnp.where((lane & 7) == h, stat, 0.0), axis=1, keepdims=True)
            near_lse = near_lse_ref[head]
            top = jnp.maximum(far_lse, near_lse)
            far_scale = jnp.exp(far_lse - top)
            near_scale = jnp.exp(near_lse - top)
            merged = far[h * 8 : (h + 1) * 8] * far_scale + near_ref[head] * near_scale
            out_ref[:, head * HD : (head + 1) * HD] = (merged / (far_scale + near_scale)).astype(
                jnp.bfloat16
            )


VMEM = pl.BlockSpec(memory_space=pltpu.VMEM)
SMEM = pl.BlockSpec(memory_space=pltpu.SMEM)


def params(mib):
    return pltpu.CompilerParams(vmem_limit_bytes=mib << 20)


def shards(
    prompt_of,
    suffix_len,
    query,
    new_key,
    new_value,
    suffix_key,
    suffix_value,
    prefix_key,
    prefix_value,
):
    place = lax.axis_index(NEAR).astype(jnp.int32).reshape(1)
    sent, *cuts = pl.pallas_call(
        prep_kernel,
        out_shape=[jax.ShapeDtypeStruct((KVH, 80, HD), jnp.bfloat16)]
        + [jax.ShapeDtypeStruct((2, PIECE, HD), jnp.bfloat16)] * 8,
        in_specs=[SMEM, SMEM, VMEM, VMEM, VMEM],
        out_specs=[VMEM] * 9,
        compiler_params=params(16),
        name="prep",
    )(place, prompt_of, query, prefix_key, prefix_value)
    held = [cuts[0]]
    for step in range(1, 8):
        held.append(lax.ppermute(cuts[step], NEAR, [(i, i ^ step) for i in range(8)]))
    swapped = [lax.ppermute(piece, "c", [(0, 1), (1, 0)]) for piece in held]
    got = lax.all_to_all(sent, "y", 0, 0, tiled=True)
    outgoing = pl.pallas_call(
        pack_kernel,
        out_shape=jax.ShapeDtypeStruct((ROWS, HD), jnp.bfloat16),
        in_specs=[VMEM],
        out_specs=VMEM,
        compiler_params=params(16),
        name="pack",
    )(got)
    arrived = lax.all_to_all(outgoing.reshape(PROMPTS, 64, HD), FAR, 0, 0, tiled=True)

    near_out, near_lse = pl.pallas_call(
        near_kernel,
        grid=(HELD,),
        out_shape=[jax.ShapeDtypeStruct((HEADS, HELD, HD), jnp.float32)] * 2,
        in_specs=[
            SMEM,
            pl.BlockSpec((1, HEADS, HD), lambda i: (i, 0, 0)),
            pl.BlockSpec((HELD, KVH * HD), lambda i: (0, 0)),
            pl.BlockSpec((HELD, KVH * HD), lambda i: (0, 0)),
            pl.BlockSpec((1, SUF, KVH * HD), lambda i: (i, 0, 0)),
            pl.BlockSpec((1, SUF, KVH * HD), lambda i: (i, 0, 0)),
        ],
        out_specs=[pl.BlockSpec((HEADS, HELD, HD), lambda i: (0, 0, 0))] * 2,
        compiler_params=params(16),
        cost_estimate=pl.CostEstimate(flops=300_000_000, bytes_accessed=4_500_000, transcendentals=65536),
        name="near",
    )(
        suffix_len,
        query.reshape(HELD, HEADS, HD),
        new_key.astype(jnp.float32),
        new_value.astype(jnp.float32),
        suffix_key,
        suffix_value,
    )

    parcel = pl.pallas_call(
        far_kernel,
        out_shape=jax.ShapeDtypeStruct((PROMPTS, 80, HD), jnp.bfloat16),
        in_specs=[VMEM] * 17,
        out_specs=VMEM,
        scratch_shapes=[
            pltpu.VMEM((16, 256, PIECE), jnp.float32),
            pltpu.VMEM((RATIO, SLOTS, HD), jnp.bfloat16),
            pltpu.VMEM((RATIO, SLOTS, HD), jnp.bfloat16),
            pltpu.VMEM((SLOTS, HD), jnp.bfloat16),
        ],
        compiler_params=params(32),
        name="far",
    )(arrived.reshape(ROWS, HD), *held, *swapped)
    back = lax.all_to_all(parcel, FAR, 0, 0, tiled=True)
    chosen = pl.pallas_call(
        select_kernel,
        out_shape=jax.ShapeDtypeStruct((KVH, 80, HD), jnp.bfloat16),
        in_specs=[VMEM] * 2,
        out_specs=VMEM,
        compiler_params=params(16),
        name="select",
    )(got, back)
    final = lax.all_to_all(chosen, "y", 0, 0, tiled=True)
    return pl.pallas_call(
        merge_kernel,
        out_shape=jax.ShapeDtypeStruct((HELD, HEADS * HD), jnp.bfloat16),
        in_specs=[VMEM] * 3,
        out_specs=VMEM,
        compiler_params=params(16),
        name="merge",
    )(final, near_out, near_lse)


def solution(mesh):
    fine = Mesh(mesh.devices.reshape(2, 8, 2, 4, 2), ALL)
    grp = ("xh", "z")
    blk = ("xl", "y", "c")
    in_specs = (
        P(ALL),
        P(ALL),
        P(ALL, None),
        P(ALL, None),
        P(ALL, None),
        P(ALL, None, None),
        P(ALL, None, None),
        P(grp, blk, None),
        P(grp, blk, None),
    )
    return jax.shard_map(
        shards, mesh=fine, in_specs=in_specs, out_specs=P(ALL, None), check_vma=False
    )
```

time: 101 us -> 117 us (1.16)
  blocking collectives: 0 us -> 44.1 us
  waiting for transfers between devices: 28.8 us -> 10 us
  local copies, waits for them, and re-layouts: 5.72 us -> 20.8 us
  starting transfers between devices: 39.3 us -> 26.4 us
  Pallas kernels: 23.7 us -> 13.5 us
  other arithmetic: 1.73 us -> 0.01 us
    all_to_all x0 -> x2, blocking collectives: none -> 44.1 us  [the longest x1 34.2 us: shards(): back = lax.all_to_all(parcel, FAR, 0, 0, tiled=True)]
    all_to_all x2, waiting for transfers between devices: 16.9 us -> 0.01 us  [the longest x1 0.01 us: shards(): lax.all_to_all(outgoing.reshape(PROMPTS, 64, HD), FAR, 0, 0, tiled=True)]
    unnamed x23 -> x61, local copies, waits for them, and re-layouts: 5.2 us -> 20.8 us
    all_to_all x2, starting transfers between devices: 25.5 us -> 14.5 us  [the longest x1 11.2 us: shards(): lax.all_to_all(outgoing.reshape(PROMPTS, 64, HD), FAR, 0, 0, tiled=True)]
    pallas_call x2 -> x3, Pallas kernels: 15.8 us -> 7.18 us  [the longest x1 5.29 us: shards(): pl.pallas_call(far_kernel, out_shape=jax.ShapeDtypeStruct((PROMPTS, 80, H...]
    ppermute x7, starting transfers between devices: 12.3 us -> 10.4 us  [shards(): lax.ppermute(cuts[step], NEAR, [(i, i ^ step) for i in range(8)])]
    concatenate x1 -> x0, other arithmetic: 1.72 us -> none  [shards(): jnp.concatenate([far_out.reshape(DEVICES, 4, 2, HD), jnp.broadcast_to(far...]
  transfers between devices with their start and end apart: 17 -> 17, of which waited for: 10 -> 4; matrix products, arithmetic and copies ran while one was open for 0% -> 0% of each run, Pallas kernels for 4% -> 4%
where the time goes in v2:
time: 117 us; the launch traced here: 115 us
  blocking collectives  44.1 us (38%)
  starting transfers between devices  26.4 us (23%)
  local copies, waits for them, and re-layouts  20.8 us (18%)
  Pallas kernels  13.5 us (12%)
  waiting for transfers between devices  10 us (9%)
    all_to_all x1, blocking collectives, shards(): back = lax.all_to_all(parcel, FAR, 0, 0, tiled=True)  34.2 us
    unnamed x61, local copies, waits for them, and re-layouts  20.8 us
    all_to_all x1, starting transfers between devices, shards(): lax.all_to_all(outgoing.reshape(PROMPTS, 64, HD), FAR, 0, 0, tiled=True)  11.2 us
    ppermute x7, starting transfers between devices, shards(): lax.ppermute(cuts[step], NEAR, [(i, i ^ step) for i in range(8)])  10.4 us
    ppermute x7, waiting for transfers between devices, shards(): lax.ppermute(cuts[step], NEAR, [(i, i ^ step) for i in range(8)])  10 us
    all_to_all x1, blocking collectives, shards(): got = lax.all_to_all(sent, 'y', 0, 0, tiled=True)  9.98 us
    pallas_call x1, Pallas kernels, shards(): pl.pallas_call(far_kernel, out_shape=jax.ShapeDtypeStruct((PROMPTS, 80, H...  5.29 us
    pallas_call x1, Pallas kernels, shards(): pl.pallas_call(near_kernel, grid=(HELD,), out_shape=[jax.ShapeDtypeStruct...  4.04 us
  transfers between devices with their start and end apart: 17, of which 4 were waited for; matrix products, arithmetic and copies ran while one was open for 0% of the time, Pallas kernels for 4%

profile of v2, /device:TPU:32, one launch (start us, length us, event | category | flops | bytes accessed | tf_op | source)
XLA Modules:
  0.0 115.0 jit_solution(8093890587664004745)
XLA Ops:
  0.0 1.0 copy-done.2
  1.0 1.0 copy-done.3
  2.1 0.8 copy-done.4
  3.6 0.8 prep.1
  4.4 10.0 %all_to_all.20.got_ref = bf16[4,80,128]{2,1,0:T(8,128)(2,1)S(1)} all-to-all(bf16[4,80,128]{2,1,0:T(8,128)(2,1)S(1)} %get-tuple-element.16), channel_id=1, replica_groups=mesh['xh'=2,'z'=8,'xl'=2,'y'=4,'c'=2] {'y'}, dimensions={0} | all-to-all | bytes 163840 | tf_op jit(solution)/shard_map/all_to_all | solution.py:288
  14.3 1.5 %pack.1 = bf16[2048,128]{1,0:T(8,128)(2,1)} custom-call(bf16[4,80,128]{2,1,0:T(8,128)(2,1)S(1)} %all_to_all.20.got_ref), custom_call_target="tpu_custom_call" | custom-call | tf_op jit(solution)/shard_map/pack/pallas_call | solution.py:289
  15.8 11.2 %all-to-all-start.1 = ((bf16[32,64,128]{2,1,0:T(8,128)(2,1)}), bf16[32,64,128]{2,1,0:T(8,128)(2,1)S(1)}, u32[]{:S(2)}, u32[]{:S(2)}) async-start(bf16[32,64,128]{2,1,0:T(8,128)(2,1)} %bitcast.1), calls=%async_computation.1 | async-start | bytes 1048576 | tf_op jit(solution)/shard_map/all_to_all | solution.py:297
  27.0 1.3 %collective-permute-start.2 = (bf16[2,256,128]{2,1,0:T(8,128)(2,1)S(1)}, bf16[2,256,128]{2,1,0:T(8,128)(2,1)S(1)}, u32[]{:S(2)}, u32[]{:S(2)}) collective-permute-start(bf16[2,256,128]{2,1,0:T(8,128)(2,1)S(1)} %get-tuple-element.20), channel_id=1, source_target_pairs={{0,6},{2,4},{4,2},{6,0},{8,14},{10,12},{12,10},{14,8},{1,7},{3,5},... | collective-permute-start | bytes 393224 | tf_op jit(solution)/shard_map/ppermute | solution.py:286
  28.3 1.5 %collective-permute-start.3 = (bf16[2,256,128]{2,1,0:T(8,128)(2,1)S(1)}, bf16[2,256,128]{2,1,0:T(8,128)(2,1)S(1)}, u32[]{:S(2)}, u32[]{:S(2)}) collective-permute-start(bf16[2,256,128]{2,1,0:T(8,128)(2,1)S(1)} %get-tuple-element.21), channel_id=1, source_target_pairs={{0,8},{2,10},{4,12},{6,14},{8,0},{10,2},{12,4},{14,6},{1,9},{3,11}... | collective-permute-start | bytes 393224 | tf_op jit(solution)/shard_map/ppermute | solution.py:286
  29.7 4.4 %collective-permute-start.5 = (bf16[2,256,128]{2,1,0:T(8,128)(2,1)S(1)}, bf16[2,256,128]{2,1,0:T(8,128)(2,1)S(1)}, u32[]{:S(2)}, u32[]{:S(2)}) collective-permute-start(bf16[2,256,128]{2,1,0:T(8,128)(2,1)S(1)} %get-tuple-element.23), channel_id=1, source_target_pairs={{0,12},{2,14},{4,8},{6,10},{8,4},{10,6},{12,0},{14,2},{1,13},{3,15... | collective-permute-start | bytes 393224 | tf_op jit(solution)/shard_map/ppermute | solution.py:286
  34.2 1.2 %collective-permute-start.6 = (bf16[2,256,128]{2,1,0:T(8,128)(2,1)S(1)}, bf16[2,256,128]{2,1,0:T(8,128)(2,1)S(1)}, u32[]{:S(2)}, u32[]{:S(2)}) collective-permute-start(bf16[2,256,128]{2,1,0:T(8,128)(2,1)S(1)} %get-tuple-element.24), channel_id=1, source_target_pairs={{0,14},{2,12},{4,10},{6,8},{8,6},{10,4},{12,2},{14,0},{1,15},{3,13... | collective-permute-start | bytes 393224 | tf_op jit(solution)/shard_map/ppermute | solution.py:286
  35.3 1.5 %collective-permute-done.3.refs_4_ = bf16[2,256,128]{2,1,0:T(8,128)(2,1)S(1)} collective-permute-done((bf16[2,256,128]{2,1,0:T(8,128)(2,1)S(1)}, bf16[2,256,128]{2,1,0:T(8,128)(2,1)S(1)}, u32[]{:S(2)}, u32[]{:S(2)}) %collective-permute-start.3) | collective-permute-done | bytes 131104 | tf_op jit(solution)/shard_map/ppermute | solution.py:286
  36.8 2.1 %collective-permute-start.1 = (bf16[2,256,128]{2,1,0:T(8,128)(2,1)S(1)}, bf16[2,256,128]{2,1,0:T(8,128)(2,1)S(1)}, u32[]{:S(2)}, u32[]{:S(2)}) collective-permute-start(bf16[2,256,128]{2,1,0:T(8,128)(2,1)S(1)} %get-tuple-element.19), channel_id=1, source_target_pairs={{0,4},{2,6},{4,0},{6,2},{8,12},{10,14},{12,8},{14,10},{1,5},{3,7},... | collective-permute-start | bytes 393224 | tf_op jit(solution)/shard_map/ppermute | solution.py:286
  39.5 4.9 %collective-permute-done.5.refs_6_ = bf16[2,256,128]{2,1,0:T(8,128)(2,1)S(1)} collective-permute-done((bf16[2,256,128]{2,1,0:T(8,128)(2,1)S(1)}, bf16[2,256,128]{2,1,0:T(8,128)(2,1)S(1)}, u32[]{:S(2)}, u32[]{:S(2)}) %collective-permute-start.5) | collective-permute-done | bytes 131104 | tf_op jit(solution)/shard_map/ppermute | solution.py:286
  44.4 3.0 %collective-permute-done.6.refs_7_ = bf16[2,256,128]{2,1,0:T(8,128)(2,1)S(1)} collective-permute-done((bf16[2,256,128]{2,1,0:T(8,128)(2,1)S(1)}, bf16[2,256,128]{2,1,0:T(8,128)(2,1)S(1)}, u32[]{:S(2)}, u32[]{:S(2)}) %collective-permute-start.6) | collective-permute-done | bytes 131104 | tf_op jit(solution)/shard_map/ppermute | solution.py:286
  55.5 0.9 copy-done.7
  56.4 0.9 copy-done.9
  57.3 0.9 copy-done.11
  58.2 0.9 copy-done.13
  59.2 0.9 copy-done.15
  60.1 0.9 copy-done.17
  61.0 0.9 copy-done.19
  61.9 0.9 copy-done.21
  62.8 0.9 copy-done.23
  63.7 0.9 copy-done.25
  64.6 5.3 %far.1 = bf16[32,80,128]{2,1,0:T(8,128)(2,1)S(1)} custom-call(bf16[2048,128]{1,0:T(8,128)(2,1)S(1)} %bitcast.7, bf16[2,256,128]{2,1,0:T(8,128)(2,1)S(1)} %get-tuple-element.17.refs_0_, bf16[2,256,128]{2,1,0:T(8,128)(2,1)S(1)} %copy-done.7, bf16[2,256,128]{2,1,0:T(8,128)(2,1)S(1)} %copy-done.9, bf16[2,256,128]{2,1,0:T(8,128)(2,1)S(1)} %collective-permute-done.2.refs_3_, ...), custom_call_target="tpu_custom_call" | custom-call | tf_op jit(solution)/shard_map/far/pallas_call | solution.py:324
  69.9 34.2 %all_to_all.21.back_ref = bf16[32,80,128]{2,1,0:T(8,128)(2,1)S(1)} all-to-all(bf16[32,80,128]{2,1,0:T(8,128)(2,1)S(1)} %far.1), channel_id=1, replica_groups=mesh['xh'=2,'z'=8,'xl'=2,'y'=4,'c'=2] {'xh','z','xl'}, dimensions={0} | all-to-all | bytes 1310720 | tf_op jit(solution)/shard_map/all_to_all | solution.py:338
  104.1 1.1 select.1
  105.2 3.3 %all-to-all-start.3 = ((bf16[4,80,128]{2,1,0:T(8,128)(2,1)}), bf16[4,80,128]{2,1,0:T(8,128)(2,1)S(1)}, u32[]{:S(2)}, u32[]{:S(2)}) async-start(bf16[4,80,128]{2,1,0:T(8,128)(2,1)} %select.1), calls=%async_computation.3 | async-start | bytes 163840 | tf_op jit(solution)/shard_map/all_to_all | solution.py:347
  108.6 1.6 %copy-done.1 = bf16[8,256,512]{2,1,0:T(8,128)(2,1)S(1)} copy-done((bf16[8,256,512]{2,1,0:T(8,128)(2,1)S(1)}, bf16[8,256,512]{2,1,0:T(8,128)(2,1)}, u32[]{:S(2)}) %copy-start.1) | copy-done | bytes 2097176
  110.2 4.0 %near.1 = (f32[32,8,128]{2,1,0:T(8,128)S(1)}, f32[32,8,128]{2,1,0:T(8,128)S(1)}) custom-call(s32[8]{0:T(128)S(1)} %copy-done.27, bf16[8,32,128]{2,1,0:T(8,128)(2,1)S(1)} %bitcast.8, f32[8,512]{1,0:T(8,128)S(1)} %convert_element_type.6.new_key_ref, f32[8,512]{1,0:T(8,128)S(1)} %convert_element_type.7.new_value_ref, bf16[8,256,512]{2,1,0:T(8,128)(2,1)S(1)} %copy-done, ...), custom_call_target="tpu_custom_call" | custom-call | flops 300000000 | bytes 4500000 | tf_op jit(solution)/shard_map/near/pallas_call | solution.py:299
  114.2 0.8 merge.1
  (73 shorter events, 9.5 us)
Async XLA Ops:
  0.0 1.0 copy-start.2
  1.0 1.0 copy-start.3
  15.8 39.7 %all-to-all-start.1 = ((bf16[32,64,128]{2,1,0:T(8,128)(2,1)}), bf16[32,64,128]{2,1,0:T(8,128)(2,1)S(1)}, u32[]{:S(2)}, u32[]{:S(2)}) async-start(bf16[32,64,128]{2,1,0:T(8,128)(2,1)} %bitcast.1), calls=%async_computation.1 | async-start | bytes 1048576 | tf_op jit(solution)/shard_map/all_to_all | solution.py:297
  27.0 8.3 %collective-permute-start.2 = (bf16[2,256,128]{2,1,0:T(8,128)(2,1)S(1)}, bf16[2,256,128]{2,1,0:T(8,128)(2,1)S(1)}, u32[]{:S(2)}, u32[]{:S(2)}) collective-permute-start(bf16[2,256,128]{2,1,0:T(8,128)(2,1)S(1)} %get-tuple-element.20), channel_id=1, source_target_pairs={{0,6},{2,4},{4,2},{6,0},{8,14},{10,12},{12,10},{14,8},{1,7},{3,5},... | collective-permute-start | bytes 393224 | tf_op jit(solution)/shard_map/ppermute | solution.py:286
  28.3 8.5 %collective-permute-start.3 = (bf16[2,256,128]{2,1,0:T(8,128)(2,1)S(1)}, bf16[2,256,128]{2,1,0:T(8,128)(2,1)S(1)}, u32[]{:S(2)}, u32[]{:S(2)}) collective-permute-start(bf16[2,256,128]{2,1,0:T(8,128)(2,1)S(1)} %get-tuple-element.21), channel_id=1, source_target_pairs={{0,8},{2,10},{4,12},{6,14},{8,0},{10,2},{12,4},{14,6},{1,9},{3,11}... | collective-permute-start | bytes 393224 | tf_op jit(solution)/shard_map/ppermute | solution.py:286
  29.7 9.8 %collective-permute-start.4 = (bf16[2,256,128]{2,1,0:T(8,128)(2,1)S(1)}, bf16[2,256,128]{2,1,0:T(8,128)(2,1)S(1)}, u32[]{:S(2)}, u32[]{:S(2)}) collective-permute-start(bf16[2,256,128]{2,1,0:T(8,128)(2,1)S(1)} %get-tuple-element.22), channel_id=1, source_target_pairs={{0,10},{2,8},{4,14},{6,12},{8,2},{10,0},{12,6},{14,4},{1,11},{3,9}... | collective-permute-start | bytes 393224 | tf_op jit(solution)/shard_map/ppermute | solution.py:286
  29.7 14.7 %collective-permute-start.5 = (bf16[2,256,128]{2,1,0:T(8,128)(2,1)S(1)}, bf16[2,256,128]{2,1,0:T(8,128)(2,1)S(1)}, u32[]{:S(2)}, u32[]{:S(2)}) collective-permute-start(bf16[2,256,128]{2,1,0:T(8,128)(2,1)S(1)} %get-tuple-element.23), channel_id=1, source_target_pairs={{0,12},{2,14},{4,8},{6,10},{8,4},{10,6},{12,0},{14,2},{1,13},{3,15... | collective-permute-start | bytes 393224 | tf_op jit(solution)/shard_map/ppermute | solution.py:286
  34.2 13.3 %collective-permute-start.6 = (bf16[2,256,128]{2,1,0:T(8,128)(2,1)S(1)}, bf16[2,256,128]{2,1,0:T(8,128)(2,1)S(1)}, u32[]{:S(2)}, u32[]{:S(2)}) collective-permute-start(bf16[2,256,128]{2,1,0:T(8,128)(2,1)S(1)} %get-tuple-element.24), channel_id=1, source_target_pairs={{0,14},{2,12},{4,10},{6,8},{8,6},{10,4},{12,2},{14,0},{1,15},{3,13... | collective-permute-start | bytes 393224 | tf_op jit(solution)/shard_map/ppermute | solution.py:286
  35.3 12.1 %collective-permute-start = (bf16[2,256,128]{2,1,0:T(8,128)(2,1)S(1)}, bf16[2,256,128]{2,1,0:T(8,128)(2,1)S(1)}, u32[]{:S(2)}, u32[]{:S(2)}) collective-permute-start(bf16[2,256,128]{2,1,0:T(8,128)(2,1)S(1)} %get-tuple-element.18), channel_id=1, source_target_pairs={{0,2},{2,0},{4,6},{6,4},{8,10},{10,8},{12,14},{14,12},{1,3},{3,1},... | collective-permute-start | bytes 393224 | tf_op jit(solution)/shard_map/ppermute | solution.py:286
  36.8 11.1 %collective-permute-start.1 = (bf16[2,256,128]{2,1,0:T(8,128)(2,1)S(1)}, bf16[2,256,128]{2,1,0:T(8,128)(2,1)S(1)}, u32[]{:S(2)}, u32[]{:S(2)}) collective-permute-start(bf16[2,256,128]{2,1,0:T(8,128)(2,1)S(1)} %get-tuple-element.19), channel_id=1, source_target_pairs={{0,4},{2,6},{4,0},{6,2},{8,12},{10,14},{12,8},{14,10},{1,5},{3,7},... | collective-permute-start | bytes 393224 | tf_op jit(solution)/shard_map/ppermute | solution.py:286
  39.5 8.5 %collective-permute-start.7 = (bf16[2,256,128]{2,1,0:T(8,128)(2,1)S(1)}, bf16[2,256,128]{2,1,0:T(8,128)(2,1)S(1)}, u32[]{:S(2)}, u32[]{:S(2)}) collective-permute-start(bf16[2,256,128]{2,1,0:T(8,128)(2,1)S(1)} %get-tuple-element.17.refs_0_), channel_id=1, source_target_pairs={{0,1},{1,0},{2,3},{3,2},{4,5},{5,4},{6,7},{7,6},{8,9},{9,8},{10,11... | collective-permute-start | bytes 393224 | tf_op jit(solution)/shard_map/ppermute | solution.py:287
  44.4 4.7 %collective-permute-start.10 = (bf16[2,256,128]{2,1,0:T(8,128)(2,1)S(1)}, bf16[2,256,128]{2,1,0:T(8,128)(2,1)S(1)}, u32[]{:S(2)}, u32[]{:S(2)}) collective-permute-start(bf16[2,256,128]{2,1,0:T(8,128)(2,1)S(1)} %collective-permute-done.2.refs_3_), channel_id=1, source_target_pairs={{0,1},{1,0},{2,3},{3,2},{4,5},{5,4},{6,7},{7,6},{8,9},{9,8},{10,11... | collective-permute-start | bytes 393224 | tf_op jit(solution)/shard_map/ppermute | solution.py:287
  47.4 3.1 %collective-permute-start.11 = (bf16[2,256,128]{2,1,0:T(8,128)(2,1)S(1)}, bf16[2,256,128]{2,1,0:T(8,128)(2,1)S(1)}, u32[]{:S(2)}, u32[]{:S(2)}) collective-permute-start(bf16[2,256,128]{2,1,0:T(8,128)(2,1)S(1)} %collective-permute-done.3.refs_4_), channel_id=1, source_target_pairs={{0,1},{1,0},{2,3},{3,2},{4,5},{5,4},{6,7},{7,6},{8,9},{9,8},{10,11... | collective-permute-start | bytes 393224 | tf_op jit(solution)/shard_map/ppermute | solution.py:287
  47.4 4.8 %collective-permute-start.12 = (bf16[2,256,128]{2,1,0:T(8,128)(2,1)S(1)}, bf16[2,256,128]{2,1,0:T(8,128)(2,1)S(1)}, u32[]{:S(2)}, u32[]{:S(2)}) collective-permute-start(bf16[2,256,128]{2,1,0:T(8,128)(2,1)S(1)} %collective-permute-done.4.refs_5_), channel_id=1, source_target_pairs={{0,1},{1,0},{2,3},{3,2},{4,5},{5,4},{6,7},{7,6},{8,9},{9,8},{10,11... | collective-permute-start | bytes 393224 | tf_op jit(solution)/shard_map/ppermute | solution.py:287
  47.9 4.9 %collective-permute-start.13 = (bf16[2,256,128]{2,1,0:T(8,128)(2,1)S(1)}, bf16[2,256,128]{2,1,0:T(8,128)(2,1)S(1)}, u32[]{:S(2)}, u32[]{:S(2)}) collective-permute-start(bf16[2,256,128]{2,1,0:T(8,128)(2,1)S(1)} %collective-permute-done.5.refs_6_), channel_id=1, source_target_pairs={{0,1},{1,0},{2,3},{3,2},{4,5},{5,4},{6,7},{7,6},{8,9},{9,8},{10,11... | collective-permute-start | bytes 393224 | tf_op jit(solution)/shard_map/ppermute | solution.py:287
  48.7 4.9 %collective-permute-start.14 = (bf16[2,256,128]{2,1,0:T(8,128)(2,1)S(1)}, bf16[2,256,128]{2,1,0:T(8,128)(2,1)S(1)}, u32[]{:S(2)}, u32[]{:S(2)}) collective-permute-start(bf16[2,256,128]{2,1,0:T(8,128)(2,1)S(1)} %collective-permute-done.6.refs_7_), channel_id=1, source_target_pairs={{0,1},{1,0},{2,3},{3,2},{4,5},{5,4},{6,7},{7,6},{8,9},{9,8},{10,11... | collective-permute-start | bytes 393224 | tf_op jit(solution)/shard_map/ppermute | solution.py:287
  49.8 4.5 %collective-permute-start.8 = (bf16[2,256,128]{2,1,0:T(8,128)(2,1)S(1)}, bf16[2,256,128]{2,1,0:T(8,128)(2,1)S(1)}, u32[]{:S(2)}, u32[]{:S(2)}) collective-permute-start(bf16[2,256,128]{2,1,0:T(8,128)(2,1)S(1)} %collective-permute-done.refs_1_), channel_id=1, source_target_pairs={{0,1},{1,0},{2,3},{3,2},{4,5},{5,4},{6,7},{7,6},{8,9},{9,8},{10,11... | collective-permute-start | bytes 393224 | tf_op jit(solution)/shard_map/ppermute | solution.py:287
  51.2 3.7 %collective-permute-start.9 = (bf16[2,256,128]{2,1,0:T(8,128)(2,1)S(1)}, bf16[2,256,128]{2,1,0:T(8,128)(2,1)S(1)}, u32[]{:S(2)}, u32[]{:S(2)}) collective-permute-start(bf16[2,256,128]{2,1,0:T(8,128)(2,1)S(1)} %collective-permute-done.1.refs_2_), channel_id=1, source_target_pairs={{0,1},{1,0},{2,3},{3,2},{4,5},{5,4},{6,7},{7,6},{8,9},{9,8},{10,11... | collective-permute-start | bytes 393224 | tf_op jit(solution)/shard_map/ppermute | solution.py:287
  55.5 0.9 copy-start.7
  56.4 0.9 copy-start.9
  57.3 0.9 copy-start.11
  58.2 0.9 copy-start.13
  59.2 0.9 copy-start.15
  62.8 0.9 copy-start.23
  63.7 0.9 copy-start.25
  64.6 43.9 %copy-start.5 = (bf16[8,4096]{1,0:T(8,128)(2,1)S(1)}, bf16[8,4096]{1,0:T(8,128)(2,1)}, u32[]{:S(2)}) copy-start(bf16[8,4096]{1,0:T(8,128)(2,1)} %query_ref.1) | copy-start | bytes 196612
  64.6 44.0 %copy-start = (bf16[8,256,512]{2,1,0:T(8,128)(2,1)S(1)}, bf16[8,256,512]{2,1,0:T(8,128)(2,1)}, u32[]{:S(2)}) copy-start(bf16[8,256,512]{2,1,0:T(8,128)(2,1)} %key_ref.3) | copy-start | bytes 6291460
  69.9 38.6 %copy-start.28 = (bf16[8,512]{1,0:T(8,128)(2,1)S(1)}, bf16[8,512]{1,0:T(8,128)(2,1)}, u32[]{:S(2)}) copy-start(bf16[8,512]{1,0:T(8,128)(2,1)} %param.12) | copy-start | bytes 24580
  69.9 38.7 %copy-start.29 = (bf16[8,512]{1,0:T(8,128)(2,1)S(1)}, bf16[8,512]{1,0:T(8,128)(2,1)}, u32[]{:S(2)}) copy-start(bf16[8,512]{1,0:T(8,128)(2,1)} %param.13) | copy-start | bytes 24580
  69.9 38.7 %copy-start.27 = (s32[8]{0:T(128)S(1)}, s32[8]{0:T(128)}, u32[]{:S(2)}) copy-start(s32[8]{0:T(128)} %len_ref.1) | copy-start | bytes 100
  105.2 9.0 %all-to-all-start.3 = ((bf16[4,80,128]{2,1,0:T(8,128)(2,1)}), bf16[4,80,128]{2,1,0:T(8,128)(2,1)S(1)}, u32[]{:S(2)}, u32[]{:S(2)}) async-start(bf16[4,80,128]{2,1,0:T(8,128)(2,1)} %select.1), calls=%async_computation.3 | async-start | bytes 163840 | tf_op jit(solution)/shard_map/all_to_all | solution.py:347
  108.6 1.6 %copy-start.1 = (bf16[8,256,512]{2,1,0:T(8,128)(2,1)S(1)}, bf16[8,256,512]{2,1,0:T(8,128)(2,1)}, u32[]{:S(2)}) copy-start(bf16[8,256,512]{2,1,0:T(8,128)(2,1)} %value_ref.3) | copy-start | bytes 6291460
  (15 other events, 10.7 us)

commit v3 on v2

--- a/solution.py
+++ b/solution.py
@@ -44,7 +44,30 @@
     return picked
 
 
-def prep_kernel(place_ref, prompt_ref, query_ref, key_ref, value_ref, send_ref, *cut_refs):
+def prep_kernel(place_ref, prompt_hbm, query_hbm, key_ref, value_ref, send_ref, *refs):
+    cut_refs = refs[:8]
+    prompt_ref, query_ref, small_sem, cut_sem = refs[8:]
+    small = [
+        pltpu.make_async_copy(prompt_hbm, prompt_ref, small_sem.at[0]),
+        pltpu.make_async_copy(query_hbm, query_ref, small_sem.at[1]),
+    ]
+    for copy in small:
+        copy.start()
+    place = place_ref[0]
+    copies = []
+    for step, cut_ref in enumerate(cut_refs):
+        target = place ^ step
+        prompt = target >> 2
+        column = pl.multiple_of((target & 3) * HD, HD)
+        for n, cache in enumerate((key_ref, value_ref)):
+            copies.append(
+                pltpu.make_async_copy(
+                    cache.at[prompt, :, pl.ds(column, HD)], cut_ref.at[n], cut_sem.at[step, n]
+                )
+            )
+            copies[-1].start()
+    for copy in small:
+        copy.wait()
     slots = slots_of(prompt_ref)
     lane = lax.broadcasted_iota(jnp.int32, (HELD, HD), 1)
     row = lax.broadcasted_iota(jnp.int32, (HELD, HD), 0)
@@ -60,16 +83,12 @@
             axis=0,
         ).astype(jnp.bfloat16)
         send_ref[y, 64:] = tags
-    place = place_ref[0]
-    for step, cut_ref in enumerate(cut_refs):
-        target = place ^ step
-        prompt = target >> 2
-        column = pl.multiple_of((target & 3) * HD, HD)
-        cut_ref[0] = key_ref[prompt, :, pl.ds(column, HD)]
-        cut_ref[1] = value_ref[prompt, :, pl.ds(column, HD)]
-
-
-def pack_kernel(got_ref, out_ref):
+    for copy in copies:
+        copy.wait()
+
+
+def pack_kernel(got_ref, *refs):
+    out_ref = refs[-1]
     held = got_ref[:, :64].reshape(256, HD)
     tags = [got_ref[y, 64:].astype(jnp.float32)[:1].astype(jnp.int32) for y in range(KVH)]
     half = lax.broadcasted_iota(jnp.int32, (1, HD), 1) < 64
@@ -136,8 +155,14 @@
 
 
 def far_kernel(query_ref, *refs):
-    pieces = refs[:16]
-    out_ref, score_ref, query_scr, mixed_scr, stat_scr = refs[16:]
+    sources = refs[:16]
+    out_ref, score_ref, query_scr, mixed_scr, stat_scr, cache_ref, sems = refs[16:]
+    copies = [
+        pltpu.make_async_copy(source, cache_ref.at[n], sems.at[n]) for n, source in enumerate(sources)
+    ]
+    for copy in copies:
+        copy.start()
+    pieces = [cache_ref.at[n] for n in range(16)]
     span = 32
     block = span * RATIO
     tokens = 16 * PIECE
@@ -162,6 +187,8 @@
         ).astype(jnp.bfloat16)
     mixed_scr[...] = jnp.zeros_like(mixed_scr)
     stat_scr[...] = jnp.zeros_like(stat_scr)
+    for copy in copies:
+        copy.wait()
 
     @pl.loop(0, (count + span - 1) // span)
     def _(index):
@@ -216,7 +243,8 @@
     return stat
 
 
-def select_kernel(got_ref, back_ref, send_ref):
+def select_kernel(got_ref, back_ref, *refs):
+    send_ref = refs[-1]
     tags = [got_ref[y, 64:].astype(jnp.float32)[8:, :1].astype(jnp.int32) for y in range(KVH)]
     lane = lax.broadcasted_iota(jnp.int32, (1, ROWS), 1)
     lane_key = ((lane >> 1) & 3) * 512 + ((lane >> 3) & 7) * 64 + (lane >> 6) * 2 + (lane & 1)
@@ -254,6 +282,8 @@
 
 VMEM = pl.BlockSpec(memory_space=pltpu.VMEM)
 SMEM = pl.BlockSpec(memory_space=pltpu.SMEM)
+ANY = pl.BlockSpec(memory_space=pl.ANY)
+HBM = pl.BlockSpec(memory_space=pltpu.HBM)
 
 
 def params(mib):
@@ -276,9 +306,15 @@
         prep_kernel,
         out_shape=[jax.ShapeDtypeStruct((KVH, 80, HD), jnp.bfloat16)]
         + [jax.ShapeDtypeStruct((2, PIECE, HD), jnp.bfloat16)] * 8,
-        in_specs=[SMEM, SMEM, VMEM, VMEM, VMEM],
+        in_specs=[SMEM, HBM, HBM, HBM, HBM],
         out_specs=[VMEM] * 9,
-        compiler_params=params(16),
+        scratch_shapes=[
+            pltpu.SMEM((HELD,), jnp.int32),
+            pltpu.VMEM((HELD, HEADS * HD), jnp.bfloat16),
+            pltpu.SemaphoreType.DMA((2,)),
+            pltpu.SemaphoreType.DMA((8, 2)),
+        ],
+        compiler_params=params(12),
         name="prep",
     )(place, prompt_of, query, prefix_key, prefix_value)
     held = [cuts[0]]
@@ -289,11 +325,11 @@
     outgoing = pl.pallas_call(
         pack_kernel,
         out_shape=jax.ShapeDtypeStruct((ROWS, HD), jnp.bfloat16),
-        in_specs=[VMEM],
+        in_specs=[VMEM] + [ANY] * 4,
         out_specs=VMEM,
-        compiler_params=params(16),
+        compiler_params=params(8),
         name="pack",
-    )(got)
+    )(got, *held[4:])
     arrived = lax.all_to_all(outgoing.reshape(PROMPTS, 64, HD), FAR, 0, 0, tiled=True)
 
     near_out, near_lse = pl.pallas_call(
@@ -309,7 +345,7 @@
             pl.BlockSpec((1, SUF, KVH * HD), lambda i: (i, 0, 0)),
         ],
         out_specs=[pl.BlockSpec((HEADS, HELD, HD), lambda i: (0, 0, 0))] * 2,
-        compiler_params=params(16),
+        compiler_params=params(12),
         cost_estimate=pl.CostEstimate(flops=300_000_000, bytes_accessed=4_500_000, transcendentals=65536),
         name="near",
     )(
@@ -324,33 +360,35 @@
     parcel = pl.pallas_call(
         far_kernel,
         out_shape=jax.ShapeDtypeStruct((PROMPTS, 80, HD), jnp.bfloat16),
-        in_specs=[VMEM] * 17,
+        in_specs=[VMEM] + [ANY] * 16,
         out_specs=VMEM,
         scratch_shapes=[
             pltpu.VMEM((16, 256, PIECE), jnp.float32),
             pltpu.VMEM((RATIO, SLOTS, HD), jnp.bfloat16),
             pltpu.VMEM((RATIO, SLOTS, HD), jnp.bfloat16),
             pltpu.VMEM((SLOTS, HD), jnp.bfloat16),
+            pltpu.VMEM((16, 2, PIECE, HD), jnp.bfloat16),
+            pltpu.SemaphoreType.DMA((16,)),
         ],
-        compiler_params=params(32),
+        compiler_params=params(16),
         name="far",
     )(arrived.reshape(ROWS, HD), *held, *swapped)
     back = lax.all_to_all(parcel, FAR, 0, 0, tiled=True)
     chosen = pl.pallas_call(
         select_kernel,
         out_shape=jax.ShapeDtypeStruct((KVH, 80, HD), jnp.bfloat16),
-        in_specs=[VMEM] * 2,
+        in_specs=[VMEM] * 2 + [ANY] * 2,
         out_specs=VMEM,
-        compiler_params=params(16),
+        compiler_params=params(8),
         name="select",
-    )(got, back)
+    )(got, back, near_out, near_lse)
     final = lax.all_to_all(chosen, "y", 0, 0, tiled=True)
     return pl.pallas_call(
         merge_kernel,
         out_shape=jax.ShapeDtypeStruct((HELD, HEADS * HD), jnp.bfloat16),
         in_specs=[VMEM] * 3,
         out_specs=VMEM,
-        compiler_params=params(16),
+        compiler_params=params(12),
         name="merge",
     )(final, near_out, near_lse)
 

time: 117 us -> 111 us (0.949)
  blocking collectives: 44.1 us -> 18.2 us
  waiting for transfers between devices: 10 us -> 19.7 us
  Pallas kernels: 13.5 us -> 20.4 us
  starting transfers between devices: 26.4 us -> 28.9 us
  other arithmetic: 0.01 us -> 1.4 us
    all_to_all x1, blocking collectives: 34.2 us -> 8.08 us  [shards(): final = lax.all_to_all(chosen, 'y', 0, 0, tiled=True)]
    all_to_all x1, waiting for transfers between devices: 0.01 us -> 14.5 us  [shards(): back = lax.all_to_all(parcel, FAR, 0, 0, tiled=True)]
    pallas_call x1, Pallas kernels: 5.29 us -> 12.8 us  [shards(): pl.pallas_call(far_kernel, out_shape=jax.ShapeDtypeStruct((PROMPTS, 80, H...]
    ppermute x7, waiting for transfers between devices: 10 us -> 4.35 us  [shards(): lax.ppermute(cuts[step], NEAR, [(i, i ^ step) for i in range(8)])]
    ppermute x7, starting transfers between devices: 10.4 us -> 11.9 us  [shards(): lax.ppermute(cuts[step], NEAR, [(i, i ^ step) for i in range(8)])]
    unnamed x61 -> x57, local copies, waits for them, and re-layouts: 20.8 us -> 21.4 us
  transfers between devices with their start and end apart: 17 -> 17, of which waited for: 4 -> 4; matrix products, arithmetic and copies ran while one was open for 0% -> 1% of each run, Pallas kernels for 4% -> 4%
where the time goes in v3:
time: 111 us; the launch traced here: 110 us
  starting transfers between devices  28.9 us (26%)
  local copies, waits for them, and re-layouts  21.4 us (19%)
  Pallas kernels  20.4 us (18%)
  waiting for transfers between devices  19.7 us (18%)
  blocking collectives  18.2 us (16%)
  other arithmetic  1.4 us (1%)
    unnamed x57, local copies, waits for them, and re-layouts  21.4 us
    all_to_all x1, waiting for transfers between devices, shards(): back = lax.all_to_all(parcel, FAR, 0, 0, tiled=True)  14.5 us
    pallas_call x1, Pallas kernels, shards(): pl.pallas_call(far_kernel, out_shape=jax.ShapeDtypeStruct((PROMPTS, 80, H...  12.8 us
    ppermute x7, starting transfers between devices, shards(): lax.ppermute(cuts[step], NEAR, [(i, i ^ step) for i in range(8)])  11.9 us
    all_to_all x1, starting transfers between devices, shards(): lax.all_to_all(outgoing.reshape(PROMPTS, 64, HD), FAR, 0, 0, tiled=True)  11.2 us
    all_to_all x1, blocking collectives, shards(): got = lax.all_to_all(sent, 'y', 0, 0, tiled=True)  10.1 us
    all_to_all x1, blocking collectives, shards(): final = lax.all_to_all(chosen, 'y', 0, 0, tiled=True)  8.08 us
    ppermute x7, waiting for transfers between devices, shards(): lax.ppermute(cuts[step], NEAR, [(i, i ^ step) for i in range(8)])  4.35 us
  transfers between devices with their start and end apart: 17, of which 4 were waited for; matrix products, arithmetic and copies ran while one was open for 1% of the time, Pallas kernels for 4%

profile of v3, /device:TPU:32, one launch (start us, length us, event | category | flops | bytes accessed | tf_op | source)
XLA Modules:
  0.0 110.1 jit_solution(17883720631184385007)
XLA Ops:
  0.0 1.0 copy-done.2
  1.0 1.0 copy-done.3
  2.1 0.8 copy-done.4
  3.6 0.8 prep.1
  4.4 1.6 %collective-permute-start = (bf16[2,256,128]{2,1,0:T(8,128)(2,1)S(1)}, bf16[2,256,128]{2,1,0:T(8,128)(2,1)S(1)}, u32[]{:S(2)}, u32[]{:S(2)}) collective-permute-start(bf16[2,256,128]{2,1,0:T(8,128)(2,1)S(1)} %get-tuple-element.17), channel_id=1, source_target_pairs={{0,8},{2,10},{4,12},{6,14},{8,0},{10,2},{12,4},{14,6},{1,9},{3,11}... | collective-permute-start | bytes 393224 | tf_op jit(solution)/shard_map/ppermute | solution.py:322
  5.9 1.5 %collective-permute-start.1 = (bf16[2,256,128]{2,1,0:T(8,128)(2,1)S(1)}, bf16[2,256,128]{2,1,0:T(8,128)(2,1)S(1)}, u32[]{:S(2)}, u32[]{:S(2)}) collective-permute-start(bf16[2,256,128]{2,1,0:T(8,128)(2,1)S(1)} %get-tuple-element.18), channel_id=1, source_target_pairs={{0,10},{2,8},{4,14},{6,12},{8,2},{10,0},{12,6},{14,4},{1,11},{3,9}... | collective-permute-start | bytes 393224 | tf_op jit(solution)/shard_map/ppermute | solution.py:322
  7.5 3.8 %collective-permute-start.2 = (bf16[2,256,128]{2,1,0:T(8,128)(2,1)S(1)}, bf16[2,256,128]{2,1,0:T(8,128)(2,1)S(1)}, u32[]{:S(2)}, u32[]{:S(2)}) collective-permute-start(bf16[2,256,128]{2,1,0:T(8,128)(2,1)S(1)} %get-tuple-element.19), channel_id=1, source_target_pairs={{0,12},{2,14},{4,8},{6,10},{8,4},{10,6},{12,0},{14,2},{1,13},{3,15... | collective-permute-start | bytes 393224 | tf_op jit(solution)/shard_map/ppermute | solution.py:322
  11.5 10.1 %all_to_all.20.got_ref = bf16[4,80,128]{2,1,0:T(8,128)(2,1)S(1)} all-to-all(bf16[4,80,128]{2,1,0:T(8,128)(2,1)S(1)} %get-tuple-element.16), channel_id=1, replica_groups=mesh['xh'=2,'z'=8,'xl'=2,'y'=4,'c'=2] {'y'}, dimensions={0} | all-to-all | bytes 163840 | tf_op jit(solution)/shard_map/all_to_all | solution.py:324
  21.6 1.5 %pack.1 = bf16[2048,128]{1,0:T(8,128)(2,1)} custom-call(bf16[4,80,128]{2,1,0:T(8,128)(2,1)S(1)} %all_to_all.20.got_ref, bf16[2,256,128]{2,1,0:T(8,128)(2,1)S(1)} %collective-permute-done.refs_0_.refs_4_, bf16[2,256,128]{2,1,0:T(8,128)(2,1)S(1)} %collective-permute-done.1.refs_1_.refs_5_, bf16[2,256,128]{2,1,0:T(8,128)(2,1)S(1)} %collective-permute-done.2.refs_2_.refs_6_, ...), custom_call_target="tpu_custom_call" | custom-call | tf_op jit(solution)/shard_map/pack/pallas_call | solution.py:325
  23.1 11.2 %all-to-all-start.1 = ((bf16[32,64,128]{2,1,0:T(8,128)(2,1)}), bf16[32,64,128]{2,1,0:T(8,128)(2,1)S(1)}, u32[]{:S(2)}, u32[]{:S(2)}) async-start(bf16[32,64,128]{2,1,0:T(8,128)(2,1)} %bitcast.1), calls=%async_computation.1 | async-start | bytes 1048576 | tf_op jit(solution)/shard_map/all_to_all | solution.py:333
  34.3 1.0 collective-permute-start.6
  35.3 3.8 %collective-permute-start.5 = (bf16[2,256,128]{2,1,0:T(8,128)(2,1)S(1)}, bf16[2,256,128]{2,1,0:T(8,128)(2,1)S(1)}, u32[]{:S(2)}, u32[]{:S(2)}) collective-permute-start(bf16[2,256,128]{2,1,0:T(8,128)(2,1)S(1)} %get-tuple-element.23), channel_id=1, source_target_pairs={{0,4},{2,6},{4,0},{6,2},{8,12},{10,14},{12,8},{14,10},{1,5},{3,7},... | collective-permute-start | bytes 393224 | tf_op jit(solution)/shard_map/ppermute | solution.py:322
  39.6 1.7 %collective-permute-done.6.refs_3_ = bf16[2,256,128]{2,1,0:T(8,128)(2,1)S(1)} collective-permute-done((bf16[2,256,128]{2,1,0:T(8,128)(2,1)S(1)}, bf16[2,256,128]{2,1,0:T(8,128)(2,1)S(1)}, u32[]{:S(2)}, u32[]{:S(2)}) %collective-permute-start.6) | collective-permute-done | bytes 131104 | tf_op jit(solution)/shard_map/ppermute | solution.py:322
  41.9 2.6 %collective-permute-done.5.refs_2_ = bf16[2,256,128]{2,1,0:T(8,128)(2,1)S(1)} collective-permute-done((bf16[2,256,128]{2,1,0:T(8,128)(2,1)S(1)}, bf16[2,256,128]{2,1,0:T(8,128)(2,1)S(1)}, u32[]{:S(2)}, u32[]{:S(2)}) %collective-permute-start.5) | collective-permute-done | bytes 131104 | tf_op jit(solution)/shard_map/ppermute | solution.py:322
  52.1 0.8 all-to-all-done.1
  52.9 0.9 copy-done.7
  53.8 0.9 copy-done.9
  54.7 0.9 copy-done.11
  55.6 0.9 copy-done.13
  56.5 0.9 copy-done.15
  57.4 0.9 copy-done.17
  58.3 0.9 copy-done.19
  59.2 0.9 copy-done.21
  60.1 0.9 copy-done.23
  61.0 0.9 copy-done.25
  61.9 12.8 %far.1 = bf16[32,80,128]{2,1,0:T(8,128)(2,1)} custom-call(bf16[2048,128]{1,0:T(8,128)(2,1)S(1)} %bitcast.7, bf16[2,256,128]{2,1,0:T(8,128)(2,1)S(1)} %get-tuple-element.21.refs_0_, bf16[2,256,128]{2,1,0:T(8,128)(2,1)S(1)} %copy-done.7, bf16[2,256,128]{2,1,0:T(8,128)(2,1)S(1)} %copy-done.9, bf16[2,256,128]{2,1,0:T(8,128)(2,1)S(1)} %collective-permute-done.6.refs_3_, ...), custom_call_target="tpu_custom_call" | custom-call | tf_op jit(solution)/shard_map/far/pallas_call | solution.py:360
  74.8 3.7 %all-to-all-start.2 = ((bf16[32,80,128]{2,1,0:T(8,128)(2,1)}), bf16[32,80,128]{2,1,0:T(8,128)(2,1)S(1)}, u32[]{:S(2)}, u32[]{:S(2)}) async-start(bf16[32,80,128]{2,1,0:T(8,128)(2,1)} %far.1), calls=%async_computation.2 | async-start | bytes 1310720 | tf_op jit(solution)/shard_map/all_to_all | solution.py:376
  79.9 1.6 %copy-done.1 = bf16[8,256,512]{2,1,0:T(8,128)(2,1)S(1)} copy-done((bf16[8,256,512]{2,1,0:T(8,128)(2,1)S(1)}, bf16[8,256,512]{2,1,0:T(8,128)(2,1)}, u32[]{:S(2)}) %copy-start.1) | copy-done | bytes 2097176
  82.2 4.0 %near.1 = (f32[32,8,128]{2,1,0:T(8,128)S(1)}, f32[32,8,128]{2,1,0:T(8,128)S(1)}) custom-call(s32[8]{0:T(128)S(1)} %copy-done.27, bf16[8,32,128]{2,1,0:T(8,128)(2,1)S(1)} %bitcast.8, f32[8,512]{1,0:T(8,128)S(1)} %convert_element_type.6.new_key_ref, f32[8,512]{1,0:T(8,128)S(1)} %convert_element_type.7.new_value_ref, bf16[8,256,512]{2,1,0:T(8,128)(2,1)S(1)} %copy-done, ...), custom_call_target="tpu_custom_call" | custom-call | flops 300000000 | bytes 4500000 | tf_op jit(solution)/shard_map/near/pallas_call | solution.py:335
  86.2 14.5 %all-to-all-done.2.back_ref = bf16[32,80,128]{2,1,0:T(8,128)(2,1)S(1)} async-done(((bf16[32,80,128]{2,1,0:T(8,128)(2,1)}), bf16[32,80,128]{2,1,0:T(8,128)(2,1)S(1)}, u32[]{:S(2)}, u32[]{:S(2)}) %all-to-all-start.2) | async-done | bytes 655392 | tf_op jit(solution)/shard_map/all_to_all | solution.py:376
  101.2 8.1 %all_to_all.21.back_ref = bf16[4,80,128]{2,1,0:T(8,128)(2,1)S(1)} all-to-all(bf16[4,80,128]{2,1,0:T(8,128)(2,1)S(1)} %select.1), channel_id=1, replica_groups=mesh['xh'=2,'z'=8,'xl'=2,'y'=4,'c'=2] {'y'}, dimensions={0} | all-to-all | bytes 163840 | tf_op jit(solution)/shard_map/all_to_all | solution.py:385
  109.3 0.8 merge.1
  (69 shorter events, 12.1 us)
Async XLA Ops:
  0.0 1.0 copy-start.2
  1.0 1.0 copy-start.3
  4.4 17.3 %collective-permute-start = (bf16[2,256,128]{2,1,0:T(8,128)(2,1)S(1)}, bf16[2,256,128]{2,1,0:T(8,128)(2,1)S(1)}, u32[]{:S(2)}, u32[]{:S(2)}) collective-permute-start(bf16[2,256,128]{2,1,0:T(8,128)(2,1)S(1)} %get-tuple-element.17), channel_id=1, source_target_pairs={{0,8},{2,10},{4,12},{6,14},{8,0},{10,2},{12,4},{14,6},{1,9},{3,11}... | collective-permute-start | bytes 393224 | tf_op jit(solution)/shard_map/ppermute | solution.py:322
  5.9 15.7 %collective-permute-start.1 = (bf16[2,256,128]{2,1,0:T(8,128)(2,1)S(1)}, bf16[2,256,128]{2,1,0:T(8,128)(2,1)S(1)}, u32[]{:S(2)}, u32[]{:S(2)}) collective-permute-start(bf16[2,256,128]{2,1,0:T(8,128)(2,1)S(1)} %get-tuple-element.18), channel_id=1, source_target_pairs={{0,10},{2,8},{4,14},{6,12},{8,2},{10,0},{12,6},{14,4},{1,11},{3,9}... | collective-permute-start | bytes 393224 | tf_op jit(solution)/shard_map/ppermute | solution.py:322
  7.5 14.1 %collective-permute-start.2 = (bf16[2,256,128]{2,1,0:T(8,128)(2,1)S(1)}, bf16[2,256,128]{2,1,0:T(8,128)(2,1)S(1)}, u32[]{:S(2)}, u32[]{:S(2)}) collective-permute-start(bf16[2,256,128]{2,1,0:T(8,128)(2,1)S(1)} %get-tuple-element.19), channel_id=1, source_target_pairs={{0,12},{2,14},{4,8},{6,10},{8,4},{10,6},{12,0},{14,2},{1,13},{3,15... | collective-permute-start | bytes 393224 | tf_op jit(solution)/shard_map/ppermute | solution.py:322
  11.3 10.3 %collective-permute-start.3 = (bf16[2,256,128]{2,1,0:T(8,128)(2,1)S(1)}, bf16[2,256,128]{2,1,0:T(8,128)(2,1)S(1)}, u32[]{:S(2)}, u32[]{:S(2)}) collective-permute-start(bf16[2,256,128]{2,1,0:T(8,128)(2,1)S(1)} %get-tuple-element.20), channel_id=1, source_target_pairs={{0,14},{2,12},{4,10},{6,8},{8,6},{10,4},{12,2},{14,0},{1,15},{3,13... | collective-permute-start | bytes 393224 | tf_op jit(solution)/shard_map/ppermute | solution.py:322
  23.1 29.8 %all-to-all-start.1 = ((bf16[32,64,128]{2,1,0:T(8,128)(2,1)}), bf16[32,64,128]{2,1,0:T(8,128)(2,1)S(1)}, u32[]{:S(2)}, u32[]{:S(2)}) async-start(bf16[32,64,128]{2,1,0:T(8,128)(2,1)} %bitcast.1), calls=%async_computation.1 | async-start | bytes 1048576 | tf_op jit(solution)/shard_map/all_to_all | solution.py:333
  34.3 7.0 %collective-permute-start.6 = (bf16[2,256,128]{2,1,0:T(8,128)(2,1)S(1)}, bf16[2,256,128]{2,1,0:T(8,128)(2,1)S(1)}, u32[]{:S(2)}, u32[]{:S(2)}) collective-permute-start(bf16[2,256,128]{2,1,0:T(8,128)(2,1)S(1)} %get-tuple-element.24), channel_id=1, source_target_pairs={{0,6},{2,4},{4,2},{6,0},{8,14},{10,12},{12,10},{14,8},{1,7},{3,5},... | collective-permute-start | bytes 393224 | tf_op jit(solution)/shard_map/ppermute | solution.py:322
  35.3 6.1 %collective-permute-start.4 = (bf16[2,256,128]{2,1,0:T(8,128)(2,1)S(1)}, bf16[2,256,128]{2,1,0:T(8,128)(2,1)S(1)}, u32[]{:S(2)}, u32[]{:S(2)}) collective-permute-start(bf16[2,256,128]{2,1,0:T(8,128)(2,1)S(1)} %get-tuple-element.22), channel_id=1, source_target_pairs={{0,2},{2,0},{4,6},{6,4},{8,10},{10,8},{12,14},{14,12},{1,3},{3,1},... | collective-permute-start | bytes 393224 | tf_op jit(solution)/shard_map/ppermute | solution.py:322
  35.3 9.2 %collective-permute-start.5 = (bf16[2,256,128]{2,1,0:T(8,128)(2,1)S(1)}, bf16[2,256,128]{2,1,0:T(8,128)(2,1)S(1)}, u32[]{:S(2)}, u32[]{:S(2)}) collective-permute-start(bf16[2,256,128]{2,1,0:T(8,128)(2,1)S(1)} %get-tuple-element.23), channel_id=1, source_target_pairs={{0,4},{2,6},{4,0},{6,2},{8,12},{10,14},{12,8},{14,10},{1,5},{3,7},... | collective-permute-start | bytes 393224 | tf_op jit(solution)/shard_map/ppermute | solution.py:322
  39.1 5.4 %collective-permute-start.7 = (bf16[2,256,128]{2,1,0:T(8,128)(2,1)S(1)}, bf16[2,256,128]{2,1,0:T(8,128)(2,1)S(1)}, u32[]{:S(2)}, u32[]{:S(2)}) collective-permute-start(bf16[2,256,128]{2,1,0:T(8,128)(2,1)S(1)} %get-tuple-element.21.refs_0_), channel_id=1, source_target_pairs={{0,1},{1,0},{2,3},{3,2},{4,5},{5,4},{6,7},{7,6},{8,9},{9,8},{10,11... | collective-permute-start | bytes 393224 | tf_op jit(solution)/shard_map/ppermute | solution.py:323
  39.1 6.5 %collective-permute-start.11 = (bf16[2,256,128]{2,1,0:T(8,128)(2,1)S(1)}, bf16[2,256,128]{2,1,0:T(8,128)(2,1)S(1)}, u32[]{:S(2)}, u32[]{:S(2)}) collective-permute-start(bf16[2,256,128]{2,1,0:T(8,128)(2,1)S(1)} %collective-permute-done.refs_0_.refs_4_), channel_id=1, source_target_pairs={{0,1},{1,0},{2,3},{3,2},{4,5},{5,4},{6,7},{7,6},{8,9},{9,8},{10,11... | collective-permute-start | bytes 393224 | tf_op jit(solution)/shard_map/ppermute | solution.py:323
  41.4 5.6 %collective-permute-start.12 = (bf16[2,256,128]{2,1,0:T(8,128)(2,1)S(1)}, bf16[2,256,128]{2,1,0:T(8,128)(2,1)S(1)}, u32[]{:S(2)}, u32[]{:S(2)}) collective-permute-start(bf16[2,256,128]{2,1,0:T(8,128)(2,1)S(1)} %collective-permute-done.1.refs_1_.refs_5_), channel_id=1, source_target_pairs={{0,1},{1,0},{2,3},{3,2},{4,5},{5,4},{6,7},{7,6},{8,9},{9,8},{10,11... | collective-permute-start | bytes 393224 | tf_op jit(solution)/shard_map/ppermute | solution.py:323
  41.4 7.4 %collective-permute-start.13 = (bf16[2,256,128]{2,1,0:T(8,128)(2,1)S(1)}, bf16[2,256,128]{2,1,0:T(8,128)(2,1)S(1)}, u32[]{:S(2)}, u32[]{:S(2)}) collective-permute-start(bf16[2,256,128]{2,1,0:T(8,128)(2,1)S(1)} %collective-permute-done.2.refs_2_.refs_6_), channel_id=1, source_target_pairs={{0,1},{1,0},{2,3},{3,2},{4,5},{5,4},{6,7},{7,6},{8,9},{9,8},{10,11... | collective-permute-start | bytes 393224 | tf_op jit(solution)/shard_map/ppermute | solution.py:323
  44.5 5.0 %collective-permute-start.14 = (bf16[2,256,128]{2,1,0:T(8,128)(2,1)S(1)}, bf16[2,256,128]{2,1,0:T(8,128)(2,1)S(1)}, u32[]{:S(2)}, u32[]{:S(2)}) collective-permute-start(bf16[2,256,128]{2,1,0:T(8,128)(2,1)S(1)} %collective-permute-done.3.refs_3_.refs_7_), channel_id=1, source_target_pairs={{0,1},{1,0},{2,3},{3,2},{4,5},{5,4},{6,7},{7,6},{8,9},{9,8},{10,11... | collective-permute-start | bytes 393224 | tf_op jit(solution)/shard_map/ppermute | solution.py:323
  45.1 5.0 %collective-permute-start.10 = (bf16[2,256,128]{2,1,0:T(8,128)(2,1)S(1)}, bf16[2,256,128]{2,1,0:T(8,128)(2,1)S(1)}, u32[]{:S(2)}, u32[]{:S(2)}) collective-permute-start(bf16[2,256,128]{2,1,0:T(8,128)(2,1)S(1)} %collective-permute-done.6.refs_3_), channel_id=1, source_target_pairs={{0,1},{1,0},{2,3},{3,2},{4,5},{5,4},{6,7},{7,6},{8,9},{9,8},{10,11... | collective-permute-start | bytes 393224 | tf_op jit(solution)/shard_map/ppermute | solution.py:323
  46.3 4.5 %collective-permute-start.8 = (bf16[2,256,128]{2,1,0:T(8,128)(2,1)S(1)}, bf16[2,256,128]{2,1,0:T(8,128)(2,1)S(1)}, u32[]{:S(2)}, u32[]{:S(2)}) collective-permute-start(bf16[2,256,128]{2,1,0:T(8,128)(2,1)S(1)} %collective-permute-done.4.refs_1_), channel_id=1, source_target_pairs={{0,1},{1,0},{2,3},{3,2},{4,5},{5,4},{6,7},{7,6},{8,9},{9,8},{10,11... | collective-permute-start | bytes 393224 | tf_op jit(solution)/shard_map/ppermute | solution.py:323
  47.6 3.8 %collective-permute-start.9 = (bf16[2,256,128]{2,1,0:T(8,128)(2,1)S(1)}, bf16[2,256,128]{2,1,0:T(8,128)(2,1)S(1)}, u32[]{:S(2)}, u32[]{:S(2)}) collective-permute-start(bf16[2,256,128]{2,1,0:T(8,128)(2,1)S(1)} %collective-permute-done.5.refs_2_), channel_id=1, source_target_pairs={{0,1},{1,0},{2,3},{3,2},{4,5},{5,4},{6,7},{7,6},{8,9},{9,8},{10,11... | collective-permute-start | bytes 393224 | tf_op jit(solution)/shard_map/ppermute | solution.py:323
  52.9 0.9 copy-start.7
  53.8 0.9 copy-start.9
  54.7 0.9 copy-start.11
  55.6 0.9 copy-start.13
  56.5 0.9 copy-start.15
  57.4 0.9 copy-start.17
  58.3 0.9 copy-start.19
  59.2 0.9 copy-start.21
  60.1 0.9 copy-start.23
  61.0 0.9 copy-start.25
  61.9 16.6 %copy-start.5 = (bf16[8,4096]{1,0:T(8,128)(2,1)S(1)}, bf16[8,4096]{1,0:T(8,128)(2,1)}, u32[]{:S(2)}) copy-start(bf16[8,4096]{1,0:T(8,128)(2,1)} %query_hbm.1) | copy-start | bytes 196612
  61.9 18.0 %copy-start = (bf16[8,256,512]{2,1,0:T(8,128)(2,1)S(1)}, bf16[8,256,512]{2,1,0:T(8,128)(2,1)}, u32[]{:S(2)}) copy-start(bf16[8,256,512]{2,1,0:T(8,128)(2,1)} %key_ref.3) | copy-start | bytes 6291460
  74.8 25.9 %all-to-all-start.2 = ((bf16[32,80,128]{2,1,0:T(8,128)(2,1)}), bf16[32,80,128]{2,1,0:T(8,128)(2,1)S(1)}, u32[]{:S(2)}, u32[]{:S(2)}) async-start(bf16[32,80,128]{2,1,0:T(8,128)(2,1)} %far.1), calls=%async_computation.2 | async-start | bytes 1310720 | tf_op jit(solution)/shard_map/all_to_all | solution.py:376
  79.9 1.6 %copy-start.1 = (bf16[8,256,512]{2,1,0:T(8,128)(2,1)S(1)}, bf16[8,256,512]{2,1,0:T(8,128)(2,1)}, u32[]{:S(2)}) copy-start(bf16[8,256,512]{2,1,0:T(8,128)(2,1)} %value_ref.3) | copy-start | bytes 6291460
  (13 other events, 8.7 us)
